TPU v7x, 128 devices: a whole 4x4x4 slice. The times are simulated.
128 devices in a mesh: lon: 32 (over z, x_lo, y), lat: 4 (over x_hi, core).
Axes of the slice: x: 4 (x_hi: 2, x_lo: 2; x = x_hi * 2 + x_lo), y: 4, z: 4, core: 2. Of those that a mesh axis runs over, the one named last changes fastest.
Arguments:
- state: float32 [2, 8, 1024, 4096], P(None, None, 'lat', 'lon'), may hold values from -6 to 6
- blocks: float32 [16384, 2, 8, 128], P(('lon', 'lat')), may hold values from -6 to 6
- dest_tile: int32 [16384, 1], P(('lon', 'lat')), may hold values from 0 to 127; in each aligned block of 128 rows (0 to 127, 128 to 255, ...) at most 2 rows name the same one
- dest_row: int32 [16384], P(('lon', 'lat')), may hold values from 0 to 255
- kappa: float32 [8, 1024, 4096], P(None, 'lat', 'lon'), may hold values from 0.02 to 0.2
- lon_speed: float32 [8, 1024, 4096], P(None, 'lat', 'lon'), may hold values from -0.5 to 0.5
- lat_speed: float32 [8, 1024, 4096], P(None, 'lat', 'lon'), may hold values from -0.5 to 0.5
- sea_mask: int32 [8, 1024, 4096], P(None, 'lat', 'lon'), may hold values 0 or 1
Outputs:
- updated: float32 [2, 8, 1024, 4096], P(None, None, 'lat', 'lon')
Inputs may be any that keep to these rules, and one draw needn't show every extreme that they name: `dest_tile`: among the 128 blocks of one analysis owner (aligned blocks of rows) no tile is named more than 2 times, and one tile is named exactly 2 times in some of them.
All inputs are finite; a program needn't handle non-finite values. No bound on the sum of `sea_mask` on one device may be relied on, other than what follows from the above.
Results may differ from a plain program's by a relative error of at most 0.000086.
Values sent between devices are 32-bit elements; how exact they have to be, the bound alone decides.
A program may use at most 128 MiB of HBM per device.

v0:
```python
import jax
import jax.numpy as jnp
from jax import lax
from jax.sharding import PartitionSpec as P

STEPS = 3


def padded(block, sides, width, periodic):
    for axis, dim in sides:
        count = lax.axis_size(axis)
        forward = [(i, i + 1) for i in range(count - 1)]
        if periodic:
            forward.append((count - 1, 0))
        backward = [(target, source) for source, target in forward]
        low = lax.ppermute(
            lax.slice_in_dim(block, block.shape[dim] - width, None, axis=dim), axis, forward
        )
        high = lax.ppermute(lax.slice_in_dim(block, 0, width, axis=dim), axis, backward)
        block = jnp.concatenate([low, block, high], axis=dim)
    return block


def advance(extended, diffusivity, zonal_speed, merid_speed, forcing):
    center = extended[:, :, 2:-2, 2:-2]
    east_cell = extended[:, :, 2:-2, 3:-1]
    west_cell = extended[:, :, 2:-2, 1:-3]
    far_east = extended[:, :, 2:-2, 4:]
    far_west = extended[:, :, 2:-2, :-4]
    north_cell = extended[:, :, 3:-1, 2:-2]
    south_cell = extended[:, :, 1:-3, 2:-2]
    far_north = extended[:, :, 4:, 2:-2]
    far_south = extended[:, :, :-4, 2:-2]
    laplace = east_cell + west_cell + north_cell + south_cell - 4.0 * center
    zonal = (8.0 * (east_cell - west_cell) - (far_east - far_west)) / 12.0
    meridional = (8.0 * (north_cell - south_cell) - (far_north - far_south)) / 12.0
    return center + diffusivity * laplace - zonal_speed * zonal - merid_speed * meridional + forcing


def body(state, blocks, dest_tile, dest_row, kappa, lon_speed, lat_speed, sea_mask):
    lon_count = lax.axis_size("lon")
    lat_count = lax.axis_size("lat")
    devices_all = lon_count * lat_count
    block_count = blocks.shape[0]
    tracers = blocks.shape[1]
    levels = blocks.shape[2]
    columns = blocks.shape[3]
    lat_rows = state.shape[2]
    capacity = max(2, (2 * block_count + devices_all - 1) // devices_all)
    targets = dest_tile[:, 0]
    one_hot = (targets[:, None] == jnp.arange(devices_all, dtype=jnp.int32)[None, :]).astype(
        jnp.int32
    )
    earlier = jnp.cumsum(one_hot, axis=0) - one_hot
    ranks = jnp.sum(earlier * one_hot, axis=1)
    slots = targets * capacity + ranks
    send_data = (
        jnp.zeros((devices_all * capacity, tracers, levels, columns), jnp.float32)
        .at[slots]
        .set(blocks)
    )
    send_rows = jnp.full((devices_all * capacity,), -1, jnp.int32).at[slots].set(dest_row)
    direct_data = send_data.reshape(devices_all, capacity, tracers, levels, columns)
    direct_rows = send_rows.reshape(devices_all, capacity)
    got_data, got_rows = (
        lax.all_to_all(direct_data, ("lon", "lat"), split_axis=0, concat_axis=0, tiled=True),
        lax.all_to_all(direct_rows, ("lon", "lat"), split_axis=0, concat_axis=0, tiled=True),
    )
    slot_total = devices_all * capacity
    flat_data = got_data.reshape(slot_total, tracers * levels * columns)
    flat_rows = got_rows.reshape(slot_total)
    selector = (flat_rows[None, :] == jnp.arange(lat_rows, dtype=jnp.int32)[:, None]).astype(
        jnp.float32
    )
    assembled = jnp.dot(selector, flat_data, precision=lax.Precision.HIGHEST)
    increment = assembled.reshape(lat_rows, tracers, levels, columns).transpose(1, 2, 0, 3)
    wet = sea_mask.astype(jnp.float32)
    diffusivity = kappa * wet
    zonal_speed = lon_speed * wet
    merid_speed = lat_speed * wet
    forcing = increment * wet / STEPS
    tracer = state
    for repeat in range(STEPS):
        lat_ext = padded(tracer, (("lat", 2),), 2, False)
        extended = padded(lat_ext, (("lon", 3),), 2, True)
        tracer = advance(extended, diffusivity, zonal_speed, merid_speed, forcing)
    return tracer


def solution(mesh):
    placed = (
        P(None, None, "lat", "lon"),
        P(("lon", "lat"), None, None, None),
        P(("lon", "lat"), None),
        P(("lon", "lat")),
        P(None, "lat", "lon"),
        P(None, "lat", "lon"),
        P(None, "lat", "lon"),
        P(None, "lat", "lon"),
    )
    return jax.shard_map(
        body, mesh=mesh, in_specs=placed, out_specs=P(None, None, "lat", "lon"), check_vma=False
    )
```

profile of v0, /device:TPU:1, one launch (start us, length us, event | category | flops | bytes accessed | tf_op | source)
XLA Modules:
  0.0 190.5 jit_solution(12517784211811352301)
XLA Ops:
  0.0 0.8 fusion.36
  0.8 0.2 reduce_window_sum.11
  1.0 0.8 select_reduce_fusion
  1.8 0.7 fusion.37
  2.5 1.1 scatter_custom_fusion
  3.6 0.8 all_to_all.9
  4.4 11.5 %all-to-all-start = ((s32[128,1,2]{2,1,0:T(1,128)}), s32[128,1,2]{2,1,0:T(1,128)S(1)}, u32[]{:S(2)}, u32[]{:S(2)}) async-start(s32[128,1,2]{2,1,0:T(1,128)} %bitcast.3), calls=%async_computation | async-start | bytes 131072 | tf_op jit(solution)/shard_map/all_to_all | solution.py:67
  15.9 1.5 broadcast_in_dim.5
  17.4 13.7 %scatter_fusion = f32[256,2,8,128]{3,2,1,0:T(8,128)} fusion(f32[256,2,8,128]{3,2,1,0:T(8,128)} %broadcast_in_dim.5, s32[128]{0:T(128)S(1)} %fusion.37, f32[128,2,8,128]{3,2,1,0:T(8,128)S(1)} %copy-done.5), kind=kCustom, calls=%fused_computation.1 | custom fusion | bytes 3146240 | tf_op jit(solution)/shard_map/scatter | solution.py:60
  31.0 0.0 all-to-all-done
  31.0 10.2 %all-to-all-start.1 = ((f32[128,2,2,8,128]{4,3,2,1,0:T(8,128)}), f32[128,2,2,8,128]{4,3,2,1,0:T(8,128)}, u32[]{:S(2)}, u32[]{:S(2)}) async-start(f32[128,2,2,8,128]{4,3,2,1,0:T(8,128)} %bitcast.6), calls=%async_computation.1 | async-start | bytes 4194304 | tf_op jit(solution)/shard_map/all_to_all | solution.py:66
  41.2 0.9 fusion.45
  42.1 3.0 %collective-permute-start.1 = (f32[2,8,2,128]{3,2,1,0:T(2,128)S(1)}, f32[2,8,2,128]{3,2,1,0:T(2,128)S(1)}, u32[]{:S(2)}, u32[]{:S(2)}) collective-permute-start(f32[2,8,2,128]{3,2,1,0:T(2,128)S(1)} %get-tuple-element.15), channel_id=1, source_target_pairs={{1,0},{2,1},{3,2},{5,4},{6,5},{7,6},{9,8},{10,9},{11,10},{13,12},{... | collective-permute-start | bytes 49160 | tf_op jit(solution)/shard_map/ppermute | solution.py:19
  45.2 0.0 copy-start.2
  45.2 4.1 %collective-permute-start = (f32[2,8,2,128]{3,2,1,0:T(2,128)S(1)}, f32[2,8,2,128]{3,2,1,0:T(2,128)S(1)}, u32[]{:S(2)}, u32[]{:S(2)}) collective-permute-start(f32[2,8,2,128]{3,2,1,0:T(2,128)S(1)} %get-tuple-element.16), channel_id=1, source_target_pairs={{0,1},{1,2},{2,3},{4,5},{5,6},{6,7},{8,9},{9,10},{10,11},{12,13},{... | collective-permute-start | bytes 49160 | tf_op jit(solution)/shard_map/ppermute | solution.py:16
  49.4 2.5 %convert_multiply_fusion = (f32[8,256,128]{2,1,0:T(8,128)S(1)}, f32[8,256,128]{2,1,0:T(8,128)S(1)}, f32[8,256,128]{2,1,0:T(8,128)S(1)}) fusion(f32[8,256,128]{2,1,0:T(8,128)} %param.12, s32[8,256,128]{2,1,0:T(8,128)} %param.15, f32[8,256,128]{2,1,0:T(8,128)} %param.13, f32[8,256,128]{2,1,0:T(8,128)} %param.14), kind=kLoop, calls=%fused_computation.93 | loop fusion | flops 1572864 | bytes 7340032 | tf_op jit(solution)/shard_map/mul | solution.py:78
  51.9 0.0 copy-start.4
  51.9 1.5 constant_dynamic-update-slice_fusion.1
  53.4 0.5 copy-done.4
  53.9 1.1 convert_element_type.7
  55.0 0.6 broadcast.57
  55.6 0.8 reduce.3
  56.4 0.1 eq.34
  56.5 10.5 %collective-permute-done.1 = f32[2,8,2,128]{3,2,1,0:T(2,128)S(1)} collective-permute-done((f32[2,8,2,128]{3,2,1,0:T(2,128)S(1)}, f32[2,8,2,128]{3,2,1,0:T(2,128)S(1)}, u32[]{:S(2)}, u32[]{:S(2)}) %collective-permute-start.1) | collective-permute-done | bytes 16416 | tf_op jit(solution)/shard_map/ppermute | solution.py:19
  67.0 1.8 pad_maximum_fusion
  68.8 2.7 %fusion.42 = (f32[2,8,260,2]{3,2,1,0:T(8,128)}, f32[2,8,260,2]{3,2,1,0:T(8,128)}) fusion(f32[2,8,260,128]{3,2,1,0:T(8,128)S(1)} %pad_maximum_fusion), kind=kLoop, calls=%fused_computation.96 | loop fusion | bytes 133120 | tf_op jit(solution)/shard_map/slice | solution.py:19
  71.5 2.5 %copy.10 = f32[2,8,260,2]{2,1,3,0:T(8,128)S(1)} copy(f32[2,8,260,2]{3,2,1,0:T(8,128)} %get-tuple-element.9) | data formatting | bytes 66560 | tf_op jit(solution)/shard_map/slice | solution.py:19
  74.0 2.5 %copy.12 = f32[2,8,260,2]{2,1,3,0:T(8,128)S(1)} copy(f32[2,8,260,2]{3,2,1,0:T(8,128)} %get-tuple-element.10) | data formatting | bytes 66560 | tf_op jit(solution)/shard_map/slice | solution.py:17
  76.5 1.2 collective-permute-start.3
  77.8 4.5 %collective-permute-start.2 = (f32[2,8,260,2]{2,1,3,0:T(8,128)S(1)}, f32[2,8,260,2]{2,1,3,0:T(8,128)S(1)}, u32[]{:S(2)}, u32[]{:S(2)}) collective-permute-start(f32[2,8,260,2]{2,1,3,0:T(8,128)S(1)} %copy.10), channel_id=1, source_target_pairs={{4,0},{8,4},{12,8},{16,12},{20,16},{24,20},{28,24},{32,28},{36,32}... | collective-permute-start | bytes 99848 | tf_op jit(solution)/shard_map/ppermute | solution.py:19
  82.3 0.6 constant_dynamic-update-slice_fusion
  82.9 0.6 collective-permute-done.2
  83.4 2.1 %copy.11 = f32[2,8,260,2]{3,2,1,0:T(8,128)} copy(f32[2,8,260,2]{2,1,3,0:T(8,128)S(1)} %collective-permute-done.2) | data formatting | bytes 66560 | tf_op jit(solution)/shard_map/ppermute | solution.py:19
  85.5 2.0 %copy.13 = f32[2,8,260,2]{3,2,1,0:T(8,128)} copy(f32[2,8,260,2]{2,1,3,0:T(8,128)S(1)} %collective-permute-done.3) | data formatting | bytes 66560 | tf_op jit(solution)/shard_map/ppermute | solution.py:16
  87.6 2.7 %reshape.20 = f32[256,2048]{1,0:T(8,128)} reshape(f32[128,2,2,8,128]{4,3,2,1,0:T(8,128)} %all-to-all-done.1) | data formatting | bytes 4194304 | tf_op jit(solution)/shard_map/reshape | solution.py:70
  90.3 3.0 %copy.15 = f32[2048,256]{1,0:T(8,128)} copy(f32[2048,256]{0,1:T(8,128)} %bitcast.27) | data formatting | bytes 4194304 | tf_op jit(solution)/shard_map/dot_general | solution.py:75
  93.3 16.1 %fusion.27 = (f32[2,8,256,128]{3,2,1,0:T(8,128)S(1)}, f32[2,8,256,128]{3,2,1,0:T(8,128)}) fusion(f32[2,8,256,128]{3,2,1,0:T(8,128)} %param.8, f32[2,8,2,128]{3,2,1,0:T(2,128)S(1)} %collective-permute-done, f32[2,8,258,128]{3,2,1,0:T(8,128)} %constant_dynamic-update-slice_fusion, f32[2,8,260,2]{3,2,1,0:T(8,128)} %copy.13, ...), kind=kOutput, calls=%fused_computation.63 | convolution fusion | flops 1629552640 | bytes 16877568 | tf_op jit(solution)/shard_map/dot_general | solution.py:75
  109.5 1.9 %collective-permute-start.5 = (f32[2,8,2,128]{3,2,1,0:T(2,128)S(1)}, f32[2,8,2,128]{3,2,1,0:T(2,128)S(1)}, u32[]{:S(2)}, u32[]{:S(2)}) collective-permute-start(f32[2,8,2,128]{3,2,1,0:T(2,128)S(1)} %get-tuple-element.13), channel_id=1, source_target_pairs={{1,0},{2,1},{3,2},{5,4},{6,5},{7,6},{9,8},{10,9},{11,10},{13,12},{... | collective-permute-start | bytes 49160 | tf_op jit(solution)/shard_map/ppermute | solution.py:19
  111.4 5.3 %collective-permute-start.4 = (f32[2,8,2,128]{3,2,1,0:T(2,128)S(1)}, f32[2,8,2,128]{3,2,1,0:T(2,128)S(1)}, u32[]{:S(2)}, u32[]{:S(2)}) collective-permute-start(f32[2,8,2,128]{3,2,1,0:T(2,128)S(1)} %get-tuple-element.14), channel_id=1, source_target_pairs={{0,1},{1,2},{2,3},{4,5},{5,6},{6,7},{8,9},{9,10},{10,11},{12,13},{... | collective-permute-start | bytes 49160 | tf_op jit(solution)/shard_map/ppermute | solution.py:16
  116.7 0.7 collective-permute-done.4
  117.4 0.2 pad_maximum_fusion.1
  117.6 2.0 %fusion.41 = (f32[2,8,260,2]{3,2,1,0:T(8,128)}, f32[2,8,260,2]{3,2,1,0:T(8,128)S(1)}) fusion(f32[2,8,260,128]{3,2,1,0:T(8,128)S(1)} %pad_maximum_fusion.1), kind=kLoop, calls=%fused_computation.95 | loop fusion | bytes 133120 | tf_op jit(solution)/shard_map/slice | solution.py:19
  119.6 2.5 %copy.16 = f32[2,8,260,2]{2,1,3,0:T(8,128)S(1)} copy(f32[2,8,260,2]{3,2,1,0:T(8,128)} %get-tuple-element.7) | data formatting | bytes 66560 | tf_op jit(solution)/shard_map/slice | solution.py:19
  122.2 6.0 %collective-permute-start.6 = (f32[2,8,260,2]{2,1,3,0:T(8,128)S(1)}, f32[2,8,260,2]{2,1,3,0:T(8,128)S(1)}, u32[]{:S(2)}, u32[]{:S(2)}) collective-permute-start(f32[2,8,260,2]{2,1,3,0:T(8,128)S(1)} %copy.16), channel_id=1, source_target_pairs={{4,0},{8,4},{12,8},{16,12},{20,16},{24,20},{28,24},{32,28},{36,32}... | collective-permute-start | bytes 99848 | tf_op jit(solution)/shard_map/ppermute | solution.py:19
  128.2 0.9 copy.18
  129.1 0.0 collective-permute-start.7
  129.2 0.2 collective-permute-done.6
  129.4 2.0 %copy.17 = f32[2,8,260,2]{3,2,1,0:T(8,128)} copy(f32[2,8,260,2]{2,1,3,0:T(8,128)S(1)} %collective-permute-done.6) | data formatting | bytes 66560 | tf_op jit(solution)/shard_map/ppermute | solution.py:19
  131.4 4.9 %collective-permute-done.7 = f32[2,8,260,2]{2,1,3,0:T(8,128)S(1)} collective-permute-done((f32[2,8,260,2]{2,1,3,0:T(8,128)S(1)}, f32[2,8,260,2]{2,1,3,0:T(8,128)S(1)}, u32[]{:S(2)}, u32[]{:S(2)}) %collective-permute-start.7) | collective-permute-done | bytes 33312 | tf_op jit(solution)/shard_map/ppermute | solution.py:16
  136.3 2.1 %copy.19 = f32[2,8,260,2]{3,2,1,0:T(8,128)} copy(f32[2,8,260,2]{2,1,3,0:T(8,128)S(1)} %collective-permute-done.7) | data formatting | bytes 66560 | tf_op jit(solution)/shard_map/ppermute | solution.py:16
  138.4 14.8 %fusion.18 = f32[2,8,256,128]{3,2,1,0:T(8,128)S(1)} fusion(f32[2,8,256,128]{3,2,1,0:T(8,128)} %get-tuple-element.21, f32[2,8,256,128]{3,2,1,0:T(8,128)} %copy-done.3, f32[2,8,2,128]{3,2,1,0:T(2,128)S(1)} %collective-permute-done.4, f32[2,8,2,128]{3,2,1,0:T(2,128)S(1)} %collective-permute-done.5, f32[2,8,260,2]{3,2,1,0:T(8,128)} %copy.19, ...), kind=kLoop, calls=%fused_computation.44 | loop fusion | flops 18874368 | bytes 9536512 | tf_op jit(solution)/shard_map/add | solution.py:37
  153.2 1.9 %collective-permute-start.9 = (f32[2,8,2,128]{3,2,1,0:T(2,128)S(1)}, f32[2,8,2,128]{3,2,1,0:T(2,128)S(1)}, u32[]{:S(2)}, u32[]{:S(2)}) collective-permute-start(f32[2,8,2,128]{3,2,1,0:T(2,128)S(1)} %get-tuple-element.11), channel_id=1, source_target_pairs={{1,0},{2,1},{3,2},{5,4},{6,5},{7,6},{9,8},{10,9},{11,10},{13,12},{... | collective-permute-start | bytes 49160 | tf_op jit(solution)/shard_map/ppermute | solution.py:19
  155.1 7.7 %collective-permute-start.8 = (f32[2,8,2,128]{3,2,1,0:T(2,128)S(1)}, f32[2,8,2,128]{3,2,1,0:T(2,128)S(1)}, u32[]{:S(2)}, u32[]{:S(2)}) collective-permute-start(f32[2,8,2,128]{3,2,1,0:T(2,128)S(1)} %get-tuple-element.12), channel_id=1, source_target_pairs={{0,1},{1,2},{2,3},{4,5},{5,6},{6,7},{8,9},{9,10},{10,11},{12,13},{... | collective-permute-start | bytes 49160 | tf_op jit(solution)/shard_map/ppermute | solution.py:16
  162.9 0.8 collective-permute-done.8
  163.7 0.2 pad_maximum_fusion.2
  163.9 2.7 %fusion.40 = (f32[2,8,260,2]{3,2,1,0:T(8,128)}, f32[2,8,260,2]{3,2,1,0:T(8,128)}) fusion(f32[2,8,260,128]{3,2,1,0:T(8,128)S(1)} %pad_maximum_fusion.2), kind=kLoop, calls=%fused_computation.94 | loop fusion | bytes 133120 | tf_op jit(solution)/shard_map/slice | solution.py:19
  166.6 2.5 %copy.20 = f32[2,8,260,2]{2,1,3,0:T(8,128)S(1)} copy(f32[2,8,260,2]{3,2,1,0:T(8,128)} %get-tuple-element.5) | data formatting | bytes 66560 | tf_op jit(solution)/shard_map/slice | solution.py:19
  169.1 0.2 collective-permute-start.10
  169.3 2.5 %copy.22 = f32[2,8,260,2]{2,1,3,0:T(8,128)S(1)} copy(f32[2,8,260,2]{3,2,1,0:T(8,128)} %get-tuple-element.6) | data formatting | bytes 66560 | tf_op jit(solution)/shard_map/slice | solution.py:17
  171.9 1.5 collective-permute-start.11
  173.4 2.0 %copy.21 = f32[2,8,260,2]{3,2,1,0:T(8,128)} copy(f32[2,8,260,2]{2,1,3,0:T(8,128)S(1)} %collective-permute-done.10) | data formatting | bytes 66560 | tf_op jit(solution)/shard_map/ppermute | solution.py:19
  175.4 3.9 %collective-permute-done.11 = f32[2,8,260,2]{2,1,3,0:T(8,128)S(1)} collective-permute-done((f32[2,8,260,2]{2,1,3,0:T(8,128)S(1)}, f32[2,8,260,2]{2,1,3,0:T(8,128)S(1)}, u32[]{:S(2)}, u32[]{:S(2)}) %collective-permute-start.11) | collective-permute-done | bytes 33312 | tf_op jit(solution)/shard_map/ppermute | solution.py:16
  179.3 2.1 %copy.23 = f32[2,8,260,2]{3,2,1,0:T(8,128)} copy(f32[2,8,260,2]{2,1,3,0:T(8,128)S(1)} %collective-permute-done.11) | data formatting | bytes 66560 | tf_op jit(solution)/shard_map/ppermute | solution.py:16
  181.3 9.1 %fusion.9 = f32[2,8,256,128]{3,2,1,0:T(8,128)} fusion(f32[2,8,256,128]{3,2,1,0:T(8,128)} %get-tuple-element.21, f32[2,8,256,128]{3,2,1,0:T(8,128)S(1)} %fusion.18, f32[2,8,2,128]{3,2,1,0:T(2,128)S(1)} %collective-permute-done.8, f32[2,8,2,128]{3,2,1,0:T(2,128)S(1)} %collective-permute-done.9, f32[2,8,260,2]{3,2,1,0:T(8,128)} %copy.23, ...), kind=kLoop, calls=%fused_computation.25 | loop fusion | flops 18874368 | bytes 9536512 | tf_op jit(solution)/shard_map/add | solution.py:37
  (17 shorter events, 0.1 us)
Async XLA Ops:
  0.0 17.4 %copy-start.5 = (f32[128,2,8,128]{3,2,1,0:T(8,128)S(1)}, f32[128,2,8,128]{3,2,1,0:T(8,128)}, u32[]{:S(2)}) copy-start(f32[128,2,8,128]{3,2,1,0:T(8,128)} %param.9) | copy-start | bytes 3145732
  4.4 26.6 %all-to-all-start = ((s32[128,1,2]{2,1,0:T(1,128)}), s32[128,1,2]{2,1,0:T(1,128)S(1)}, u32[]{:S(2)}, u32[]{:S(2)}) async-start(s32[128,1,2]{2,1,0:T(1,128)} %bitcast.3), calls=%async_computation | async-start | bytes 131072 | tf_op jit(solution)/shard_map/all_to_all | solution.py:67
  31.0 56.6 %all-to-all-start.1 = ((f32[128,2,2,8,128]{4,3,2,1,0:T(8,128)}), f32[128,2,2,8,128]{4,3,2,1,0:T(8,128)}, u32[]{:S(2)}, u32[]{:S(2)}) async-start(f32[128,2,2,8,128]{4,3,2,1,0:T(8,128)} %bitcast.6), calls=%async_computation.1 | async-start | bytes 4194304 | tf_op jit(solution)/shard_map/all_to_all | solution.py:66
  42.1 24.9 %collective-permute-start.1 = (f32[2,8,2,128]{3,2,1,0:T(2,128)S(1)}, f32[2,8,2,128]{3,2,1,0:T(2,128)S(1)}, u32[]{:S(2)}, u32[]{:S(2)}) collective-permute-start(f32[2,8,2,128]{3,2,1,0:T(2,128)S(1)} %get-tuple-element.15), channel_id=1, source_target_pairs={{1,0},{2,1},{3,2},{5,4},{6,5},{7,6},{9,8},{10,9},{11,10},{13,12},{... | collective-permute-start | bytes 49160 | tf_op jit(solution)/shard_map/ppermute | solution.py:19
  45.2 6.7 %copy-start.2 = (f32[2,8,256,128]{3,2,1,0:T(8,128)S(1)}, f32[2,8,256,128]{3,2,1,0:T(8,128)}, u32[]{:S(2)}) copy-start(f32[2,8,256,128]{3,2,1,0:T(8,128)} %param.8) | copy-start | bytes 6291460
  45.2 21.8 %collective-permute-start = (f32[2,8,2,128]{3,2,1,0:T(2,128)S(1)}, f32[2,8,2,128]{3,2,1,0:T(2,128)S(1)}, u32[]{:S(2)}, u32[]{:S(2)}) collective-permute-start(f32[2,8,2,128]{3,2,1,0:T(2,128)S(1)} %get-tuple-element.16), channel_id=1, source_target_pairs={{0,1},{1,2},{2,3},{4,5},{5,6},{6,7},{8,9},{9,10},{10,11},{12,13},{... | collective-permute-start | bytes 49160 | tf_op jit(solution)/shard_map/ppermute | solution.py:16
  51.9 41.4 %copy-start = (f32[8,256,128]{2,1,0:T(8,128)}, f32[8,256,128]{2,1,0:T(8,128)S(1)}, u32[]{:S(2)}) copy-start(f32[8,256,128]{2,1,0:T(8,128)S(1)} %get-tuple-element.18) | copy-start | bytes 3145732
  51.9 41.4 %copy-start.1 = (f32[8,256,128]{2,1,0:T(8,128)}, f32[8,256,128]{2,1,0:T(8,128)S(1)}, u32[]{:S(2)}) copy-start(f32[8,256,128]{2,1,0:T(8,128)S(1)} %get-tuple-element.19) | copy-start | bytes 3145732
  51.9 2.0 %copy-start.4 = (s32[8,256,128]{2,1,0:T(8,128)S(1)}, s32[8,256,128]{2,1,0:T(8,128)}, u32[]{:S(2)}) copy-start(s32[8,256,128]{2,1,0:T(8,128)} %param.15) | copy-start | bytes 3145732
  76.5 9.0 %collective-permute-start.3 = (f32[2,8,260,2]{2,1,3,0:T(8,128)S(1)}, f32[2,8,260,2]{2,1,3,0:T(8,128)S(1)}, u32[]{:S(2)}, u32[]{:S(2)}) collective-permute-start(f32[2,8,260,2]{2,1,3,0:T(8,128)S(1)} %copy.12), channel_id=1, source_target_pairs={{0,4},{4,8},{8,12},{12,16},{16,20},{20,24},{24,28},{28,32},{32,36}... | collective-permute-start | bytes 99848 | tf_op jit(solution)/shard_map/ppermute | solution.py:16
  77.8 5.7 %collective-permute-start.2 = (f32[2,8,260,2]{2,1,3,0:T(8,128)S(1)}, f32[2,8,260,2]{2,1,3,0:T(8,128)S(1)}, u32[]{:S(2)}, u32[]{:S(2)}) collective-permute-start(f32[2,8,260,2]{2,1,3,0:T(8,128)S(1)} %copy.10), channel_id=1, source_target_pairs={{4,0},{8,4},{12,8},{16,12},{20,16},{24,20},{28,24},{32,28},{36,32}... | collective-permute-start | bytes 99848 | tf_op jit(solution)/shard_map/ppermute | solution.py:19
  109.4 8.1 %copy-start.3 = (f32[2,8,256,128]{3,2,1,0:T(8,128)}, f32[2,8,256,128]{3,2,1,0:T(8,128)S(1)}, u32[]{:S(2)}) copy-start(f32[2,8,256,128]{3,2,1,0:T(8,128)S(1)} %get-tuple-element.20) | copy-start | bytes 6291460
  109.5 7.3 %collective-permute-start.5 = (f32[2,8,2,128]{3,2,1,0:T(2,128)S(1)}, f32[2,8,2,128]{3,2,1,0:T(2,128)S(1)}, u32[]{:S(2)}, u32[]{:S(2)}) collective-permute-start(f32[2,8,2,128]{3,2,1,0:T(2,128)S(1)} %get-tuple-element.13), channel_id=1, source_target_pairs={{1,0},{2,1},{3,2},{5,4},{6,5},{7,6},{9,8},{10,9},{11,10},{13,12},{... | collective-permute-start | bytes 49160 | tf_op jit(solution)/shard_map/ppermute | solution.py:19
  111.4 6.0 %collective-permute-start.4 = (f32[2,8,2,128]{3,2,1,0:T(2,128)S(1)}, f32[2,8,2,128]{3,2,1,0:T(2,128)S(1)}, u32[]{:S(2)}, u32[]{:S(2)}) collective-permute-start(f32[2,8,2,128]{3,2,1,0:T(2,128)S(1)} %get-tuple-element.14), channel_id=1, source_target_pairs={{0,1},{1,2},{2,3},{4,5},{5,6},{6,7},{8,9},{9,10},{10,11},{12,13},{... | collective-permute-start | bytes 49160 | tf_op jit(solution)/shard_map/ppermute | solution.py:16
  122.2 7.2 %collective-permute-start.6 = (f32[2,8,260,2]{2,1,3,0:T(8,128)S(1)}, f32[2,8,260,2]{2,1,3,0:T(8,128)S(1)}, u32[]{:S(2)}, u32[]{:S(2)}) collective-permute-start(f32[2,8,260,2]{2,1,3,0:T(8,128)S(1)} %copy.16), channel_id=1, source_target_pairs={{4,0},{8,4},{12,8},{16,12},{20,16},{24,20},{28,24},{32,28},{36,32}... | collective-permute-start | bytes 99848 | tf_op jit(solution)/shard_map/ppermute | solution.py:19
  129.1 7.2 %collective-permute-start.7 = (f32[2,8,260,2]{2,1,3,0:T(8,128)S(1)}, f32[2,8,260,2]{2,1,3,0:T(8,128)S(1)}, u32[]{:S(2)}, u32[]{:S(2)}) collective-permute-start(f32[2,8,260,2]{2,1,3,0:T(8,128)S(1)} %copy.18), channel_id=1, source_target_pairs={{0,4},{4,8},{8,12},{12,16},{16,20},{20,24},{24,28},{28,32},{32,36}... | collective-permute-start | bytes 99848 | tf_op jit(solution)/shard_map/ppermute | solution.py:16
  153.2 9.7 %collective-permute-start.9 = (f32[2,8,2,128]{3,2,1,0:T(2,128)S(1)}, f32[2,8,2,128]{3,2,1,0:T(2,128)S(1)}, u32[]{:S(2)}, u32[]{:S(2)}) collective-permute-start(f32[2,8,2,128]{3,2,1,0:T(2,128)S(1)} %get-tuple-element.11), channel_id=1, source_target_pairs={{1,0},{2,1},{3,2},{5,4},{6,5},{7,6},{9,8},{10,9},{11,10},{13,12},{... | collective-permute-start | bytes 49160 | tf_op jit(solution)/shard_map/ppermute | solution.py:19
  155.1 8.6 %collective-permute-start.8 = (f32[2,8,2,128]{3,2,1,0:T(2,128)S(1)}, f32[2,8,2,128]{3,2,1,0:T(2,128)S(1)}, u32[]{:S(2)}, u32[]{:S(2)}) collective-permute-start(f32[2,8,2,128]{3,2,1,0:T(2,128)S(1)} %get-tuple-element.12), channel_id=1, source_target_pairs={{0,1},{1,2},{2,3},{4,5},{5,6},{6,7},{8,9},{9,10},{10,11},{12,13},{... | collective-permute-start | bytes 49160 | tf_op jit(solution)/shard_map/ppermute | solution.py:16
  169.1 4.3 %collective-permute-start.10 = (f32[2,8,260,2]{2,1,3,0:T(8,128)S(1)}, f32[2,8,260,2]{2,1,3,0:T(8,128)S(1)}, u32[]{:S(2)}, u32[]{:S(2)}) collective-permute-start(f32[2,8,260,2]{2,1,3,0:T(8,128)S(1)} %copy.20), channel_id=1, source_target_pairs={{4,0},{8,4},{12,8},{16,12},{20,16},{24,20},{28,24},{32,28},{36,32}... | collective-permute-start | bytes 99848 | tf_op jit(solution)/shard_map/ppermute | solution.py:19
  171.9 7.4 %collective-permute-start.11 = (f32[2,8,260,2]{2,1,3,0:T(8,128)S(1)}, f32[2,8,260,2]{2,1,3,0:T(8,128)S(1)}, u32[]{:S(2)}, u32[]{:S(2)}) collective-permute-start(f32[2,8,260,2]{2,1,3,0:T(8,128)S(1)} %copy.22), channel_id=1, source_target_pairs={{0,4},{4,8},{8,12},{12,16},{16,20},{20,24},{24,28},{28,32},{32,36}... | collective-permute-start | bytes 99848 | tf_op jit(solution)/shard_map/ppermute | solution.py:16
where the time goes:
time: 193 us; the launch traced here: 190 us
  local copies, waits for them, and re-layouts  60.3 us (31%)
  starting transfers between devices  59.4 us (31%)
  other arithmetic  32.8 us (17%)
  waiting for transfers between devices  21.6 us (11%)
  matrix products  16.1 us (8%)
    add x2, other arithmetic, advance(): center + diffusivity * laplace - zonal_speed * zonal  23.9 us
    ppermute x6, starting transfers between devices, padded(): lax.ppermute(lax.slice_in_dim(block, block.shape[dim] - width, None, axis...  20 us
    ppermute x6, starting transfers between devices, padded(): lax.ppermute(lax.slice_in_dim(block, 0, width, axis=dim), axis, backward)  17.7 us
    dot_general x1, matrix products, body(): assembled = jnp.dot(selector, flat_data, precision=lax.Precision.HIGHEST)  16.1 us
    slice x9, local copies, waits for them, and re-layouts, padded(): lax.slice_in_dim(block, 0, width, axis=dim)  15.9 us
    scatter x1, local copies, waits for them, and re-layouts, body(): send_data = jnp.zeros((devices_all * capacity, tracers, levels, columns),...  13.7 us
    all_to_all x1, starting transfers between devices, body(): lax.all_to_all(direct_rows, ('lon', 'lat'), split_axis=0, concat_axis=0,...  11.5 us
    ppermute x6, waiting for transfers between devices, padded(): lax.ppermute(lax.slice_in_dim(block, 0, width, axis=dim), axis, backward)  11.3 us
  transfers between devices with their start and end apart: 14, of which 7 were waited for; matrix products, arithmetic and copies ran while one was open for 23% of the time, Pallas kernels for 0%

commit v1 on v0

v1 whole, which is shorter than its diff:
```python
import functools

import jax
import jax.numpy as jnp
from jax import lax
from jax.experimental import pallas as pl
from jax.experimental.pallas import tpu as pltpu
from jax.sharding import PartitionSpec as P

MESH = pl.DeviceIdType.MESH
STEPS = 3
HALO = 8
BLOCK = 32
STRIDE = 37


def roll(x, amount):
    amount = amount % 128
    return x if amount == 0 else pltpu.roll(x, amount, 1)


def kernel(
    state, blocks, tile_at, row_at, kappa, lon_speed, lat_speed, mask, out,
    tile_ref, row_ref, q0, q1, q2, part, force, diff, zonal, merid, wet, held, table, table_s, plan, meta_out, meta_in,
    send, recv, lon_out, lon_in, load_sem, table_sem, send_sem, recv_sem, halo_send, halo_recv, out_sem,
):
    tracers, levels = send.shape[0], kappa.shape[0]
    rows = kappa.shape[1]
    lon, lat = lax.axis_index("lon"), lax.axis_index("lat")
    me = lon * 4 + lat

    moves = (
        (tile_at, tile_ref), (row_at, row_ref), (blocks, held), (state, q0.at[:, pl.ds(HALO, rows)]),
        (kappa, diff), (lon_speed, zonal), (lat_speed, merid), (mask, wet),
    )
    loads = [pltpu.make_async_copy(src, dst, load_sem.at[k]) for k, (src, dst) in enumerate(moves)]
    for copy in loads:
        copy.start()

    def partner(i):
        target = (me + i * STRIDE) % 128
        return (target // 4, target % 4)

    barrier = pltpu.get_barrier_semaphore()

    def greet(i, carry):
        pl.semaphore_signal(barrier, inc=1, device_id=partner(i), device_id_type=MESH)
        return carry

    lax.fori_loop(1, 128, greet, 0)
    loads[0].wait()
    loads[1].wait()

    tile_of = lax.broadcasted_iota(jnp.int32, (128, 128), 0)
    number = lax.broadcasted_iota(jnp.int32, (128, 128), 1)
    lane = number
    named = tile_ref[...] == tile_of
    first = jnp.min(jnp.where(named, number, 128), axis=1, keepdims=True)
    last = jnp.max(jnp.where(named, number, -1), axis=1, keepdims=True)
    row_f = row_ref[...].astype(jnp.float32)
    first_row = jnp.sum(jnp.where(number == first, row_f, 0.0), axis=1, keepdims=True)
    last_row = jnp.sum(jnp.where(number == last, row_f, 0.0), axis=1, keepdims=True)
    first_row = jnp.where(last >= 0, first_row, -1.0)
    last_row = jnp.where(last > first, last_row, -1.0)
    plan[...] = jnp.where(lane == 0, first_row, last_row)
    slots = jnp.where(lane == 0, jnp.minimum(first, 127), jnp.maximum(last, 0))
    table[...] = jnp.transpose(slots)[:8]
    to_scalars = pltpu.make_async_copy(table, table_s, table_sem)
    to_scalars.start()
    loads[2].wait()
    to_scalars.wait()

    def pack(i, carry):
        target = (me + i * STRIDE) % 128
        meta_out[i] = plan[pl.ds(target, 1), :]
        for s in range(2):
            block = held[table_s[s, target]]
            for t in range(tracers):
                send[t, i, pl.ds(s * levels, levels)] = block[t * levels : (t + 1) * levels]
        return carry

    lax.fori_loop(0, 128, pack, 0)

    pl.semaphore_wait(barrier, 127)

    def post(i, carry):
        pltpu.make_async_remote_copy(
            src_ref=meta_out.at[i], dst_ref=meta_in.at[i], send_sem=send_sem.at[tracers], recv_sem=recv_sem.at[tracers],
            device_id=partner(i), device_id_type=MESH,
        ).start()
        return carry

    lax.fori_loop(1, 128, post, 0)
    for t in range(tracers):

        def post_blocks(i, carry):
            pltpu.make_async_remote_copy(
                src_ref=send.at[t, i], dst_ref=recv.at[t, i], send_sem=send_sem.at[t], recv_sem=recv_sem.at[t],
                device_id=partner(i), device_id_type=MESH,
            ).start()
            return carry

        lax.fori_loop(1, 128, post_blocks, 0)
    meta_in[0] = meta_out[0]
    for t in range(tracers):
        recv[t, 0] = send[t, 0]

    east, west = ((lon + 1) % 32, lat), ((lon + 31) % 32, lat)
    wide = lax.broadcasted_iota(jnp.int32, (8, 128), 1)

    def edges(values, packed, k):
        return jnp.where(wide // 4 == k, roll(values, 4 * k + 2), packed)

    def halo_copies(q, step):
        many = q.shape[0]
        copies = []
        for d, device in enumerate((east, west)):
            copies.append(pltpu.make_async_remote_copy(
                src_ref=lon_out.at[step], dst_ref=lon_in.at[step, d], send_sem=halo_send.at[step, d],
                recv_sem=halo_recv.at[step, d], device_id=device, device_id_type=MESH,
            ))
        north = pltpu.make_async_remote_copy(
            src_ref=q.at[:, pl.ds(rows, HALO)], dst_ref=q.at[:, pl.ds(0, HALO)], send_sem=halo_send.at[step, 2],
            recv_sem=halo_recv.at[step, 2], device_id=(lon, jnp.minimum(lat + 1, 3)), device_id_type=MESH,
        )
        south = pltpu.make_async_remote_copy(
            src_ref=q.at[:, pl.ds(HALO, HALO)], dst_ref=q.at[:, pl.ds(rows + HALO, HALO)], send_sem=halo_send.at[step, 3],
            recv_sem=halo_recv.at[step, 3], device_id=(lon, jnp.maximum(lat - 1, 0)), device_id_type=MESH,
        )
        return copies, north, south

    def start_halos(q, step):
        copies, north, south = halo_copies(q, step)
        for copy in copies:
            copy.start()

        @pl.when(lat < 3)
        def _():
            north.start()

        @pl.when(lat > 0)
        def _():
            south.start()

    def wait_halos(q, step):
        copies, north, south = halo_copies(q, step)
        for copy in copies:
            copy.wait()

        @pl.when(lat < 3)
        def _():
            north.wait_send()
            south.wait_recv()

        @pl.when(lat > 0)
        def _():
            south.wait_send()
            north.wait_recv()

    blank = jnp.zeros((HALO, 128), jnp.float32)

    @pl.when(lat == 0)
    def _():
        for q in (q0, q1, q2):
            for n in range(q.shape[0]):
                q[n, pl.ds(0, HALO)] = blank

    @pl.when(lat == 3)
    def _():
        for q in (q0, q1, q2):
            for n in range(q.shape[0]):
                q[n, pl.ds(rows + HALO, HALO)] = blank

    loads[3].wait()

    def state_edges(n, carry):
        packed = blank
        for k in range(rows // 8):
            packed = edges(q0[n, pl.ds(HALO + 8 * k, 8)], packed, k)
        lon_out[0, n] = packed
        return carry

    lax.fori_loop(0, tracers * levels, state_edges, 0)
    start_halos(q0, 0)

    for copy in loads[4:]:
        copy.wait()

    def scale(n, carry):
        for b in range(rows // BLOCK):
            at = (n, pl.ds(b * BLOCK, BLOCK))
            sea = wet[at].astype(jnp.float32)
            diff[at] = diff[at] * sea
            zonal[at] = zonal[at] * sea * (1.0 / 12.0)
            merid[at] = merid[at] * sea * (1.0 / 12.0)
        return carry

    lax.fori_loop(0, levels, scale, 0)

    lanes = lax.broadcasted_iota(jnp.int32, (BLOCK, 128), 1)

    def stencil(q, step, n, level, b):
        start = HALO + b * BLOCK
        here = q[n, pl.ds(start, BLOCK)]
        beside = jnp.where(wide % 4 < 2, lon_in[step, 0, n], lon_in[step, 1, n])
        side = jnp.concatenate([roll(beside, 126 - 4 * (b * (BLOCK // 8) + k)) for k in range(BLOCK // 8)], axis=0)
        east_cell = roll(jnp.where(lanes == 0, side, here), 127)
        far_east = roll(jnp.where(lanes < 2, side, here), 126)
        west_cell = roll(jnp.where(lanes == 127, side, here), 1)
        far_west = roll(jnp.where(lanes >= 126, side, here), 2)
        north_cell = q[n, pl.ds(start + 1, BLOCK)]
        south_cell = q[n, pl.ds(start - 1, BLOCK)]
        far_north = q[n, pl.ds(start + 2, BLOCK)]
        far_south = q[n, pl.ds(start - 2, BLOCK)]
        at = (level, pl.ds(b * BLOCK, BLOCK))
        laplace = (east_cell + west_cell) + (north_cell + south_cell) - 4.0 * here
        along = 8.0 * (east_cell - west_cell) - (far_east - far_west)
        across = 8.0 * (north_cell - south_cell) - (far_north - far_south)
        return here + diff[at] * laplace - zonal[at] * along - merid[at] * across

    wait_halos(q0, 0)

    def first_step(n, carry):
        for b in range(rows // BLOCK):
            part[n, pl.ds(b * BLOCK, BLOCK)] = stencil(q0, 0, n, n % levels, b)
        return carry

    lax.fori_loop(0, tracers * levels, first_step, 0)

    def arrived(t, ref, back):
        a = ref.at[t, pl.ds(1, 127)] if t < tracers else ref.at[pl.ds(1, 127)]
        pltpu.make_async_copy(a, a, back.at[t]).wait()

    arrived(tracers, meta_in, recv_sem)
    rows_of = jnp.transpose(meta_in[:, 0, :])
    grid_row = lax.broadcasted_iota(jnp.int32, (rows, 128), 0).astype(jnp.float32)
    selector = jnp.concatenate(
        [jnp.where(grid_row == rows_of[s : s + 1], 1.0, 0.0).astype(jnp.bfloat16) for s in range(2)], axis=1
    )

    for t in range(tracers):
        arrived(t, recv, recv_sem)
        flat = recv.at[t].reshape(129 * 2 * levels, 128)

        def assemble(l, carry):
            data = jnp.concatenate([flat[pl.ds(s * levels + l, 128, stride=2 * levels), :] for s in range(2)], axis=0)
            high = data.astype(jnp.bfloat16)
            rest = data - high.astype(jnp.float32)
            middle = rest.astype(jnp.bfloat16)
            low = (rest - middle.astype(jnp.float32)).astype(jnp.bfloat16)
            total = jnp.dot(selector, low, preferred_element_type=jnp.float32)
            total += jnp.dot(selector, middle, preferred_element_type=jnp.float32)
            total += jnp.dot(selector, high, preferred_element_type=jnp.float32)
            n = t * levels + l
            packed = blank
            sea = wet[l].astype(jnp.float32)
            forcing = total * sea * (1.0 / STEPS)
            force[n] = forcing
            q1[n, pl.ds(HALO, rows)] = part[n] + forcing
            for k in range(rows // 8):
                packed = edges(q1[n, pl.ds(HALO + 8 * k, 8)], packed, k)
            lon_out[1, n] = packed
            return carry

        lax.fori_loop(0, levels, assemble, 0)

    start_halos(q1, 1)
    wait_halos(q1, 1)

    def second_step(n, carry):
        packed = blank
        for b in range(rows // BLOCK):
            fresh = stencil(q1, 1, n, n % levels, b) + force[n, pl.ds(b * BLOCK, BLOCK)]
            q2[n, pl.ds(HALO + b * BLOCK, BLOCK)] = fresh
            for k in range(BLOCK // 8):
                packed = edges(fresh[8 * k : 8 * k + 8], packed, b * (BLOCK // 8) + k)
        lon_out[2, n] = packed
        return carry

    lax.fori_loop(0, tracers * levels, second_step, 0)
    start_halos(q2, 2)
    wait_halos(q2, 2)

    def third_step(n, carry):
        for b in range(rows // BLOCK):
            part[n, pl.ds(b * BLOCK, BLOCK)] = (
                stencil(q2, 2, n, n % levels, b) + force[n, pl.ds(b * BLOCK, BLOCK)]
            )
        return carry

    lax.fori_loop(0, tracers * levels, third_step, 0)
    store = pltpu.make_async_copy(part, out, out_sem)
    store.start()
    store.wait()
    for t in range(tracers):
        arrived(t, send, send_sem)
    arrived(tracers, meta_out, send_sem)


def body(state, blocks, dest_tile, dest_row, kappa, lon_speed, lat_speed, sea_mask):
    tracers, levels, rows, columns = state.shape
    fields = tracers * levels
    tall = (fields, rows + 2 * HALO, columns)
    flat = (fields, rows, columns)
    f32, i32 = jnp.float32, jnp.int32
    anywhere = pl.BlockSpec(memory_space=pltpu.HBM)
    dma, vmem = pltpu.SemaphoreType.DMA, pltpu.VMEM
    result = pl.pallas_call(
        kernel,
        out_shape=jax.ShapeDtypeStruct(flat, f32),
        in_specs=[anywhere] * 8,
        out_specs=anywhere,
        scratch_shapes=[
            vmem((1, 128), i32), vmem((1, 128), i32),
            vmem(tall, f32), vmem(tall, f32), vmem(tall, f32), vmem(flat, f32), vmem(flat, f32),
            vmem(kappa.shape, f32), vmem(kappa.shape, f32), vmem(kappa.shape, f32), vmem(kappa.shape, i32),
            vmem((128, fields, columns), f32), vmem((8, 128), i32), pltpu.SMEM((8, 128), i32),
            vmem((128, 128), f32), vmem((128, 1, 128), f32), vmem((128, 1, 128), f32),
            vmem((tracers, 128, 2 * levels, columns), f32), vmem((tracers, 129, 2 * levels, columns), f32),
            vmem((STEPS, fields, 8, 128), f32), vmem((STEPS, 2, fields, 8, 128), f32),
            dma((8,)), dma, dma((tracers + 1,)), dma((tracers + 1,)),
            dma((STEPS, 4)), dma((STEPS, 4)), dma,
        ],
        compiler_params=pltpu.CompilerParams(
            collective_id=0, has_side_effects=True, vmem_limit_bytes=48 << 20
        ),
    )(
        state.reshape(flat), blocks.reshape(128, fields, columns), dest_tile.reshape(1, 128), dest_row.reshape(1, 128),
        kappa, lon_speed, lat_speed, sea_mask,
    )
    return result.reshape(state.shape)


def solution(mesh):
    placed = (
        P(None, None, "lat", "lon"),
        P(("lon", "lat"), None, None, None),
        P(("lon", "lat"), None),
        P(("lon", "lat")),
        P(None, "lat", "lon"),
        P(None, "lat", "lon"),
        P(None, "lat", "lon"),
        P(None, "lat", "lon"),
    )
    return jax.shard_map(
        body, mesh=mesh, in_specs=placed, out_specs=P(None, None, "lat", "lon"), check_vma=False
    )
```

time: 193 us -> 91.2 us (0.47); the launches traced: 190 us -> 90.8 us
  Pallas kernels: 0 us -> 80.3 us
  starting transfers between devices: 59.4 us -> 0 us
  local copies, waits for them, and re-layouts: 60.3 us -> 10.5 us
  other arithmetic: 32.8 us -> 0 us
  waiting for transfers between devices: 21.6 us -> 0 us
  matrix products: 16.1 us -> 0 us
    pallas_call x0 -> x1, Pallas kernels: none -> 80.3 us  [body(): pl.pallas_call(kernel, out_shape=jax.ShapeDtypeStruct(flat, f32), in_spec...]
    ppermute x12 -> x0, starting transfers between devices: 37.7 us -> none  [the longest x6 20 us: padded(): lax.ppermute(lax.slice_in_dim(block, block.shape[dim] - width, None, axis...]
    add x2 -> x0, other arithmetic: 23.9 us -> none  [advance(): center + diffusivity * laplace - zonal_speed * zonal]
    slice x12 -> x0, local copies, waits for them, and re-layouts: 21.9 us -> none  [the longest x9 15.9 us: padded(): lax.slice_in_dim(block, 0, width, axis=dim)]
    all_to_all x2 -> x0, starting transfers between devices: 21.7 us -> none  [the longest x1 11.5 us: body(): lax.all_to_all(direct_rows, ('lon', 'lat'), split_axis=0, concat_axis=0,...]
    ppermute x12 -> x0, waiting for transfers between devices: 21.6 us -> none  [the longest x6 11.3 us: padded(): lax.ppermute(lax.slice_in_dim(block, 0, width, axis=dim), axis, backward)]
    dot_general x1 -> x0, matrix products: 16.1 us -> none  [body(): assembled = jnp.dot(selector, flat_data, precision=lax.Precision.HIGHEST)]
    scatter x2 -> x0, local copies, waits for them, and re-layouts: 14.8 us -> none  [the longest x1 13.7 us: body(): send_data = jnp.zeros((devices_all * capacity, tracers, levels, columns),...]
  transfers between devices with their start and end apart: 14 -> 0, of which waited for: 7 -> 0; matrix products, arithmetic and copies ran while one was open for 23% -> 0% of each run, Pallas kernels for 0% -> 0%
where the time goes in v1:
time: 91.2 us; the launch traced here: 90.8 us
  Pallas kernels  80.3 us (88%)
  local copies, waits for them, and re-layouts  10.5 us (12%)
    pallas_call x1, Pallas kernels, body(): pl.pallas_call(kernel, out_shape=jax.ShapeDtypeStruct(flat, f32), in_spec...  80.3 us
    unnamed x15, local copies, waits for them, and re-layouts  10.5 us

profile of v1, /device:TPU:1, one launch (start us, length us, event | category | flops | bytes accessed | tf_op | source)
XLA Modules:
  0.0 90.8 jit_solution(320865964123616982)
XLA Ops:
  0.0 0.0 copy-start
  0.0 1.2 %copy-done = f32[128,2,8,128]{3,2,1,0:T(8,128)S(1)} copy-done((f32[128,2,8,128]{3,2,1,0:T(8,128)S(1)}, f32[128,2,8,128]{3,2,1,0:T(8,128)}, u32[]{:S(2)}) %copy-start) | copy-done | bytes 1048600
  1.2 0.0 copy-start.1
  1.2 1.2 %copy-done.1 = f32[8,256,128]{2,1,0:T(8,128)S(1)} copy-done((f32[8,256,128]{2,1,0:T(8,128)S(1)}, f32[8,256,128]{2,1,0:T(8,128)}, u32[]{:S(2)}) %copy-start.1) | copy-done | bytes 1048600
  2.5 0.0 copy-start.2
  2.5 1.2 %copy-done.2 = f32[8,256,128]{2,1,0:T(8,128)S(1)} copy-done((f32[8,256,128]{2,1,0:T(8,128)S(1)}, f32[8,256,128]{2,1,0:T(8,128)}, u32[]{:S(2)}) %copy-start.2) | copy-done | bytes 1048600
  3.7 0.0 copy-start.3
  3.7 1.2 %copy-done.3 = f32[8,256,128]{2,1,0:T(8,128)S(1)} copy-done((f32[8,256,128]{2,1,0:T(8,128)S(1)}, f32[8,256,128]{2,1,0:T(8,128)}, u32[]{:S(2)}) %copy-start.3) | copy-done | bytes 1048600
  4.9 0.0 copy-start.4
  4.9 1.2 %copy-done.4 = s32[8,256,128]{2,1,0:T(8,128)S(1)} copy-done((s32[8,256,128]{2,1,0:T(8,128)S(1)}, s32[8,256,128]{2,1,0:T(8,128)}, u32[]{:S(2)}) %copy-start.4) | copy-done | bytes 1048600
  6.1 0.0 copy-start.5
  6.1 0.7 copy-done.5
  6.8 0.0 copy-start.6
  6.8 0.7 copy-done.6
  7.4 80.3 %shard_map.82 = f32[16,256,128]{2,1,0:T(8,128)} custom-call(f32[16,256,128]{2,1,0:T(8,128)} %bitcast.9, f32[128,16,128]{2,1,0:T(8,128)S(1)} %bitcast.5, s32[1,128]{1,0:T(1,128)S(1)} %bitcast.6, s32[1,128]{1,0:T(1,128)S(1)} %bitcast.7, f32[8,256,128]{2,1,0:T(8,128)S(1)} %copy-done.1, f32[8,256,128]{2,1,0:T(8,128)S(1)} %copy-done.2, ...), custom_call_target="tpu_custom_call" | custom-call | tf_op jit(solution)/shard_map/pallas_call | solution.py:308
  87.7 3.1 %copy.10 = f32[2,8,256,128]{3,2,1,0:T(8,128)} copy(f32[2,8,256,128]{3,2,1,0:T(8,128)} %bitcast.8) | data formatting | bytes 4194304
Async XLA Ops:
  0.0 1.2 %copy-start = (f32[128,2,8,128]{3,2,1,0:T(8,128)S(1)}, f32[128,2,8,128]{3,2,1,0:T(8,128)}, u32[]{:S(2)}) copy-start(f32[128,2,8,128]{3,2,1,0:T(8,128)} %param.9) | copy-start | bytes 3145732
  1.2 1.2 %copy-start.1 = (f32[8,256,128]{2,1,0:T(8,128)S(1)}, f32[8,256,128]{2,1,0:T(8,128)}, u32[]{:S(2)}) copy-start(f32[8,256,128]{2,1,0:T(8,128)} %kappa.1) | copy-start | bytes 3145732
  2.5 1.2 %copy-start.2 = (f32[8,256,128]{2,1,0:T(8,128)S(1)}, f32[8,256,128]{2,1,0:T(8,128)}, u32[]{:S(2)}) copy-start(f32[8,256,128]{2,1,0:T(8,128)} %lon_speed.1) | copy-start | bytes 3145732
  3.7 1.2 %copy-start.3 = (f32[8,256,128]{2,1,0:T(8,128)S(1)}, f32[8,256,128]{2,1,0:T(8,128)}, u32[]{:S(2)}) copy-start(f32[8,256,128]{2,1,0:T(8,128)} %lat_speed.1) | copy-start | bytes 3145732
  4.9 1.2 %copy-start.4 = (s32[8,256,128]{2,1,0:T(8,128)S(1)}, s32[8,256,128]{2,1,0:T(8,128)}, u32[]{:S(2)}) copy-start(s32[8,256,128]{2,1,0:T(8,128)} %mask.1) | copy-start | bytes 3145732
  6.1 0.7 copy-start.5
  6.8 0.7 copy-start.6

commit v2 on v0

v2 whole, which is shorter than its diff:
```python
import jax
import jax.numpy as jnp
from jax import lax
from jax.experimental import pallas as pl
from jax.experimental.pallas import tpu as pltpu
from jax.sharding import PartitionSpec as P

MESH = pl.DeviceIdType.MESH
STEPS = 3
BANDS = 8
PARTNERS = 64
STRIDE = 27
SLOTS = 2
PIECE = 40
PAD = 8
EDGE = 2


def roll(x, amount):
    amount = amount % 128
    return x if amount == 0 else pltpu.roll(x, amount, 1)


def kernel(
    state, blocks, tile_at, row_at, kappa, lon_speed, lat_speed, mask, out,
    tile_ref, row_ref, held, table, table_s, plan, send, relay, recv,
    raw_state, raw_diff, raw_zonal, raw_merid, raw_wet, raw_force, scaled,
    q0, q1, q2, part, force, diff, zonal, merid, wet, lon_out, lon_in, lat_out, lat_in,
    load_sem, table_sem, core_send, core_recv, send_sem, recv_sem, halo_send, halo_recv, out_sem,
):
    levels, rows, columns = kappa.shape
    fields = state.shape[0]
    depth = rows // BANDS
    used = SLOTS * fields + 1
    lon, lat = lax.axis_index("lon"), lax.axis_index("lat")
    core = lat % 2
    me = lon * 2 + lat // 2
    other = (lon, lat + 1 - 2 * core)

    def partner(i):
        target = (me + i * STRIDE) % PARTNERS
        return (target // 2, (target % 2) * 2 + core)

    moves = (
        (tile_at, tile_ref), (row_at, row_ref), (blocks, held), (state, raw_state.at[pl.ds(0, fields)]),
        (kappa, raw_diff.at[pl.ds(0, levels)]), (lon_speed, raw_zonal.at[pl.ds(0, levels)]),
        (lat_speed, raw_merid.at[pl.ds(0, levels)]), (mask, raw_wet),
    )
    loads = [pltpu.make_async_copy(src, dst, load_sem.at[k]) for k, (src, dst) in enumerate(moves)]
    for copy in loads:
        copy.start()

    barrier = pltpu.get_barrier_semaphore()
    for device in (other, (lon, 3 - lat)):
        pl.semaphore_signal(barrier, inc=1, device_id=device, device_id_type=MESH)

    def greet(i, carry):
        pl.semaphore_signal(barrier, inc=1, device_id=partner(i), device_id_type=MESH)
        return carry

    lax.fori_loop(1, PARTNERS, greet, 0)
    loads[0].wait()
    loads[1].wait()

    tile_of = lax.broadcasted_iota(jnp.int32, (128, 128), 0)
    number = lax.broadcasted_iota(jnp.int32, (128, 128), 1)
    named = tile_ref[...] == tile_of
    first = jnp.min(jnp.where(named, number, 128), axis=1, keepdims=True)
    last = jnp.max(jnp.where(named, number, -1), axis=1, keepdims=True)
    row_f = row_ref[...].astype(jnp.float32)
    first_row = jnp.sum(jnp.where(number == first, row_f, 0.0), axis=1, keepdims=True)
    last_row = jnp.sum(jnp.where(number == last, row_f, 0.0), axis=1, keepdims=True)
    first_row = jnp.where(last >= 0, first_row, -1.0)
    last_row = jnp.where(last > first, last_row, -1.0)
    plan[...] = jnp.where(number == 0, first_row, last_row)
    slots = jnp.where(number == 0, jnp.minimum(first, 127), jnp.maximum(last, 0))
    table[...] = jnp.transpose(slots)[:8]
    to_scalars = pltpu.make_async_copy(table, table_s, table_sem)
    to_scalars.start()
    loads[2].wait()
    to_scalars.wait()

    def pack(i, carry):
        target = (me + i * STRIDE) % PARTNERS
        for h in range(2):
            tile = (target // 2) * 4 + (target % 2) * 2 + (core if h == 0 else 1 - core)
            for s in range(SLOTS):
                send[h, i, pl.ds(s * fields, fields)] = held[table_s[s, tile]]
            send[h, i, pl.ds(SLOTS * fields, 1)] = plan[pl.ds(tile, 1), :]
        return carry

    lax.fori_loop(0, PARTNERS, pack, 0)

    pl.semaphore_wait(barrier, PARTNERS + 1)
    across = pltpu.make_async_remote_copy(
        src_ref=send.at[1, :, pl.ds(0, used)], dst_ref=relay.at[:, pl.ds(0, used)],
        send_sem=core_send, recv_sem=core_recv, device_id=other, device_id_type=MESH,
    )
    across.start()

    def post(h):
        def one(i, carry):
            src = send.at[0, i] if h == 0 else relay.at[i]
            pltpu.make_async_remote_copy(
                src_ref=src.at[pl.ds(0, used)], dst_ref=recv.at[h * PARTNERS + i, pl.ds(0, used)],
                send_sem=send_sem.at[h], recv_sem=recv_sem.at[h], device_id=partner(i), device_id_type=MESH,
            ).start()
            return carry

        lax.fori_loop(1, PARTNERS, one, 0)

    post(0)
    recv[0] = send[0, 0]

    def turned(ref, r):
        flat = ref.reshape(ref.shape[0] * rows, columns)
        taken = []
        for b in range(BANDS):
            if ref.shape[0] > fields:
                taken.append(flat[pl.ds(b * depth + r, fields, stride=rows), :])
            else:
                level = flat[pl.ds(b * depth + r, levels, stride=rows), :]
                taken += [level] * (fields // levels)
        return jnp.transpose(jnp.concatenate(taken, axis=0))

    def sweep(count, unroll, step):
        def some(i, carry):
            for k in range(unroll):
                step(i * unroll + k)
            return carry

        lax.fori_loop(0, count // unroll, some, 0)

    inner = pl.ds(PAD, columns)
    loads[3].wait()

    def turn_state(r):
        q0[r + EDGE, inner] = turned(raw_state, r)

    sweep(depth, 4, turn_state)
    across.wait()
    recv[PARTNERS] = relay[0]
    post(1)

    east, west = ((lon + 1) % 32, lat), ((lon + 31) % 32, lat)
    lanes = lax.broadcasted_iota(jnp.int32, (8, 128), 1)
    width = 128 // BANDS
    many = columns // 8

    def halo_copies(step):
        def copy(src, dst, k, device):
            return pltpu.make_async_remote_copy(
                src_ref=src, dst_ref=dst, send_sem=halo_send.at[step, k], recv_sem=halo_recv.at[step, k],
                device_id=device, device_id_type=MESH,
            )

        return (
            copy(lon_out.at[step, 0], lon_in.at[step, 0], 0, east),
            copy(lon_out.at[step, 1], lon_in.at[step, 1], 1, west),
            copy(lat_out.at[step, 0], lat_in.at[step, 0], 2, (lon, jnp.minimum(lat + 1, 3))),
            copy(lat_out.at[step, 1], lat_in.at[step, 1], 3, (lon, jnp.maximum(lat - 1, 0))),
        )

    def start_halos(q, step):
        for k in range(EDGE):
            for half in range(2):
                up, down = jnp.zeros((8, 128), jnp.float32), jnp.zeros((8, 128), jnp.float32)
                for g in range(BANDS):
                    at = pl.ds(PAD + 8 * (half * BANDS + g), 8)
                    top, bottom = q[depth + k, at], q[EDGE + k, at]
                    q[k, at] = roll(top, width)
                    q[EDGE + depth + k, at] = roll(bottom, -width)
                    up = jnp.where(lanes // width == g, roll(top, width * (g + 1)), up)
                    down = jnp.where(lanes // width == g, roll(bottom, width * g), down)
                lat_out[step, 0, pl.ds(8 * (2 * k + half), 8)] = up
                lat_out[step, 1, pl.ds(8 * (2 * k + half), 8)] = down
        for r in range(depth):
            lon_out[step, 0, pl.ds(EDGE * r, EDGE)] = q[EDGE + r, pl.ds(PAD + columns - EDGE, EDGE)]
            lon_out[step, 1, pl.ds(EDGE * r, EDGE)] = q[EDGE + r, pl.ds(PAD, EDGE)]
        to_east, to_west, to_north, to_south = halo_copies(step)
        to_east.start()
        to_west.start()

        @pl.when(lat < 3)
        def _():
            to_north.start()

        @pl.when(lat > 0)
        def _():
            to_south.start()

    def wait_halos(q, step):
        to_east, to_west, to_north, to_south = halo_copies(step)
        to_east.wait()
        to_west.wait()

        @pl.when(lat < 3)
        def _():
            to_north.wait_send()
            to_south.wait_recv()

        @pl.when(lat > 0)
        def _():
            to_south.wait_send()
            to_north.wait_recv()

        for r in range(depth):
            q[EDGE + r, pl.ds(PAD - EDGE, EDGE)] = lon_in[step, 0, pl.ds(EDGE * r, EDGE)]
            q[EDGE + r, pl.ds(PAD + columns, EDGE)] = lon_in[step, 1, pl.ds(EDGE * r, EDGE)]
        for k in range(EDGE):
            for half in range(2):
                below = lat_in[step, 0, pl.ds(8 * (2 * k + half), 8)]
                above = lat_in[step, 1, pl.ds(8 * (2 * k + half), 8)]
                for g in range(BANDS):
                    at = pl.ds(PAD + 8 * (half * BANDS + g), 8)
                    q[k, at] = jnp.where(lanes < width, roll(below, -width * g), q[k, at])
                    n = EDGE + depth + k
                    q[n, at] = jnp.where(lanes >= 128 - width, roll(above, -width * (g + 1)), q[n, at])

    blank = jnp.zeros(lat_in.shape[2:], jnp.float32)
    for step in range(STEPS):

        @pl.when(lat == 0)
        def _():
            lat_in[step, 0] = blank

        @pl.when(lat == 3)
        def _():
            lat_in[step, 1] = blank

    start_halos(q0, 0)

    for copy in loads[4:]:
        copy.wait()

    def scale(n, carry):
        for b in range(rows // 32):
            at = (n, pl.ds(b * 32, 32))
            sea = raw_wet[at].astype(jnp.float32)
            raw_diff[at] = raw_diff[at] * sea
            raw_zonal[at] = raw_zonal[at] * sea * (1.0 / 12.0)
            raw_merid[at] = raw_merid[at] * sea * (1.0 / 12.0)
            scaled[at] = sea * (1.0 / STEPS)
        return carry

    lax.fori_loop(0, levels, scale, 0)
    for raw, ref in ((raw_diff, diff), (raw_zonal, zonal), (raw_merid, merid), (scaled, wet)):

        def turn(r):
            ref[r] = turned(raw, r)

        sweep(depth, 4, turn)

    def stencil(q, r, start, size):
        n, here_at = r + EDGE, pl.ds(PAD + start, size)
        here = q[n, here_at]
        east_cell, west_cell = q[n, pl.ds(PAD + start + 1, size)], q[n, pl.ds(PAD + start - 1, size)]
        far_east, far_west = q[n, pl.ds(PAD + start + 2, size)], q[n, pl.ds(PAD + start - 2, size)]
        north_cell, south_cell = q[n + 1, here_at], q[n - 1, here_at]
        far_north, far_south = q[n + 2, here_at], q[n - 2, here_at]
        at = (r, pl.ds(start, size))
        laplace = (east_cell + west_cell) + (north_cell + south_cell) - 4.0 * here
        along = 8.0 * (east_cell - west_cell) - (far_east - far_west)
        across = 8.0 * (north_cell - south_cell) - (far_north - far_south)
        return here + diff[at] * laplace - zonal[at] * along - merid[at] * across

    whole = [(32 * b, 32) for b in range(columns // 32)]
    middle = [(8, 32), (40, 32), (72, 32), (104, 16)]
    ends = [(0, 8), (columns - 8, 8)]

    wait_halos(q0, 0)

    def first_step(r):
        for start, size in whole:
            part[r, pl.ds(start, size)] = stencil(q0, r, start, size)

    sweep(depth, 2, first_step)

    for h in range(2):
        a = recv.at[pl.ds(h * PARTNERS + 1, PARTNERS - 1), pl.ds(0, used)]
        pltpu.make_async_copy(a, a, recv_sem.at[h]).wait()
    flat = recv.reshape(recv.shape[0] * PIECE, columns)
    rows_of = jnp.transpose(flat[pl.ds(SLOTS * fields, 128, stride=PIECE), :])
    grid_row = lax.broadcasted_iota(jnp.int32, (rows, 128), 0).astype(jnp.float32)
    selector = jnp.concatenate(
        [jnp.where(grid_row == rows_of[s : s + 1], 1.0, 0.0).astype(jnp.bfloat16) for s in range(SLOTS)], axis=1
    )

    def assemble(n):
        data = jnp.concatenate([flat[pl.ds(s * fields + n, 128, stride=PIECE), :] for s in range(SLOTS)], axis=0)
        high = data.astype(jnp.bfloat16)
        rest = (data - high.astype(jnp.float32)).astype(jnp.bfloat16)
        both = jnp.dot(selector, jnp.concatenate([high, rest], axis=1), preferred_element_type=jnp.float32)
        raw_force[n] = both[:, :columns] + both[:, columns:]

    sweep(fields, 2, assemble)

    def add_forcing(r):
        forcing = turned(raw_force, r) * wet[r]
        force[r] = forcing
        q1[r + EDGE, inner] = part[r] + forcing

    sweep(depth, 4, add_forcing)

    def advance(q, r, start, size):
        return stencil(q, r, start, size) + force[r, pl.ds(start, size)]

    start_halos(q1, 1)

    def second_inside(r):
        for start, size in middle:
            q2[r + 2 * EDGE, pl.ds(PAD + start, size)] = advance(q1, r + EDGE, start, size)

    sweep(depth - 2 * EDGE, 2, second_inside)
    wait_halos(q1, 1)

    def second_ends(r):
        for start, size in ends:
            q2[r + 2 * EDGE, pl.ds(PAD + start, size)] = advance(q1, r + EDGE, start, size)

    sweep(depth - 2 * EDGE, 4, second_ends)
    for r in (0, 1, depth - 2, depth - 1):
        for start, size in whole:
            q2[r + EDGE, pl.ds(PAD + start, size)] = advance(q1, r, start, size)

    start_halos(q2, 2)

    def third_inside(r):
        for start, size in middle:
            part[r + EDGE, pl.ds(start, size)] = advance(q2, r + EDGE, start, size)

    sweep(depth - 2 * EDGE, 2, third_inside)
    wait_halos(q2, 2)
    result = raw_state.reshape(raw_state.shape[0] * rows, columns)

    def finish(r, spans):
        for start, size in spans:
            part[r, pl.ds(start, size)] = advance(q2, r, start, size)
        back = jnp.transpose(part[r])
        for b in range(BANDS):
            result[pl.ds(b * depth + r, fields, stride=rows), :] = back[b * fields : (b + 1) * fields]

    sweep(depth - 2 * EDGE, 4, lambda r: finish(r + EDGE, ends))
    for r in (0, 1, depth - 2, depth - 1):
        finish(r, whole)
    store = pltpu.make_async_copy(raw_state.at[pl.ds(0, fields)], out, out_sem)
    store.start()
    for h in range(2):
        a = recv.at[pl.ds(h * PARTNERS + 1, PARTNERS - 1), pl.ds(0, used)]
        pltpu.make_async_copy(a, a, send_sem.at[h]).wait()
    store.wait()


def body(state, blocks, dest_tile, dest_row, kappa, lon_speed, lat_speed, sea_mask):
    tracers, levels, rows, columns = state.shape
    fields, depth = tracers * levels, rows // BANDS
    flat = (fields, rows, columns)
    f32, i32 = jnp.float32, jnp.int32
    anywhere = pl.BlockSpec(memory_space=pltpu.HBM)
    dma, vmem = pltpu.SemaphoreType.DMA, pltpu.VMEM
    tall = vmem((depth + 2 * EDGE, columns + 2 * PAD, 128), f32)
    turned = vmem((depth, columns, 128), f32)
    raw, coarse = vmem((fields + 1, rows, columns), f32), vmem((levels + 1, rows, columns), f32)
    result = pl.pallas_call(
        kernel,
        out_shape=jax.ShapeDtypeStruct(flat, f32),
        in_specs=[anywhere] * 8,
        out_specs=anywhere,
        scratch_shapes=[
            vmem((1, 128), i32), vmem((1, 128), i32), vmem((128, fields, columns), f32),
            vmem((8, 128), i32), pltpu.SMEM((8, 128), i32), vmem((128, 128), f32),
            vmem((2, PARTNERS, PIECE, columns), f32), vmem((PARTNERS, PIECE, columns), f32),
            vmem((2 * PARTNERS + 1, PIECE, columns), f32),
            raw, coarse, coarse, coarse, vmem((levels, rows, columns), i32), raw, coarse,
            tall, tall, tall, turned, turned, turned, turned, turned, turned,
            vmem((STEPS, 2, EDGE * depth, 128), f32), vmem((STEPS, 2, EDGE * depth, 128), f32),
            vmem((STEPS, 2, 16 * EDGE, 128), f32), vmem((STEPS, 2, 16 * EDGE, 128), f32),
            dma((8,)), dma, dma, dma, dma((2,)), dma((2,)), dma((STEPS, 4)), dma((STEPS, 4)), dma,
        ],
        compiler_params=pltpu.CompilerParams(
            collective_id=0, has_side_effects=True, vmem_limit_bytes=63 << 20
        ),
    )(
        state.reshape(flat), blocks.reshape(128, fields, columns), dest_tile.reshape(1, 128), dest_row.reshape(1, 128),
        kappa, lon_speed, lat_speed, sea_mask,
    )
    return result.reshape(state.shape)


def solution(mesh):
    placed = (
        P(None, None, "lat", "lon"),
        P(("lon", "lat"), None, None, None),
        P(("lon", "lat"), None),
        P(("lon", "lat")),
        P(None, "lat", "lon"),
        P(None, "lat", "lon"),
        P(None, "lat", "lon"),
        P(None, "lat", "lon"),
    )
    return jax.shard_map(
        body, mesh=mesh, in_specs=placed, out_specs=P(None, None, "lat", "lon"), check_vma=False
    )
```

time: 193 us -> 60.8 us (0.32); the launches traced: 190 us -> 60.7 us
  starting transfers between devices: 59.4 us -> 0 us
  Pallas kernels: 0 us -> 57.6 us
  local copies, waits for them, and re-layouts: 60.3 us -> 3.11 us
  other arithmetic: 32.8 us -> 0 us
  waiting for transfers between devices: 21.6 us -> 0 us
  matrix products: 16.1 us -> 0 us
    pallas_call x0 -> x1, Pallas kernels: none -> 57.6 us  [body(): pl.pallas_call(kernel, out_shape=jax.ShapeDtypeStruct(flat, f32), in_spec...]
    ppermute x12 -> x0, starting transfers between devices: 37.7 us -> none  [the longest x6 20 us: padded(): lax.ppermute(lax.slice_in_dim(block, block.shape[dim] - width, None, axis...]
    add x2 -> x0, other arithmetic: 23.9 us -> none  [advance(): center + diffusivity * laplace - zonal_speed * zonal]
    slice x12 -> x0, local copies, waits for them, and re-layouts: 21.9 us -> none  [the longest x9 15.9 us: padded(): lax.slice_in_dim(block, 0, width, axis=dim)]
    all_to_all x2 -> x0, starting transfers between devices: 21.7 us -> none  [the longest x1 11.5 us: body(): lax.all_to_all(direct_rows, ('lon', 'lat'), split_axis=0, concat_axis=0,...]
    ppermute x12 -> x0, waiting for transfers between devices: 21.6 us -> none  [the longest x6 11.3 us: padded(): lax.ppermute(lax.slice_in_dim(block, 0, width, axis=dim), axis, backward)]
    dot_general x1 -> x0, matrix products: 16.1 us -> none  [body(): assembled = jnp.dot(selector, flat_data, precision=lax.Precision.HIGHEST)]
    scatter x2 -> x0, local copies, waits for them, and re-layouts: 14.8 us -> none  [the longest x1 13.7 us: body(): send_data = jnp.zeros((devices_all * capacity, tracers, levels, columns),...]
  transfers between devices with their start and end apart: 14 -> 0, of which waited for: 7 -> 0; matrix products, arithmetic and copies ran while one was open for 23% -> 0% of each run, Pallas kernels for 0% -> 0%
where the time goes in v2:
time: 60.8 us; the launch traced here: 60.7 us
  Pallas kernels  57.6 us (95%)
  local copies, waits for them, and re-layouts  3.11 us (5%)
    pallas_call x1, Pallas kernels, body(): pl.pallas_call(kernel, out_shape=jax.ShapeDtypeStruct(flat, f32), in_spec...  57.6 us
    unnamed x1, local copies, waits for them, and re-layouts  3.11 us

profile of v2, /device:TPU:1, one launch (start us, length us, event | category | flops | bytes accessed | tf_op | source)
XLA Modules:
  0.0 60.7 jit_solution(15643930324017873647)
XLA Ops:
  0.0 57.6 %shard_map.82 = f32[16,256,128]{2,1,0:T(8,128)} custom-call(f32[16,256,128]{2,1,0:T(8,128)} %bitcast.6, f32[128,16,128]{2,1,0:T(8,128)} %bitcast.7, s32[1,128]{1,0:T(1,128)} %bitcast.8, s32[1,128]{1,0:T(1,128)} %bitcast.9, f32[8,256,128]{2,1,0:T(8,128)} %kappa.1, f32[8,256,128]{2,1,0:T(8,128)} %lon_speed.1, f32[8,256,128]{2,1,0:T(8,128)} %lat_speed.1, ...), custom_call_target="tpu_custom_call" | custom-call | tf_op jit(solution)/shard_map/pallas_call | solution.py:364
  57.6 3.1 %copy.10 = f32[2,8,256,128]{3,2,1,0:T(8,128)} copy(f32[2,8,256,128]{3,2,1,0:T(8,128)} %bitcast.5) | data formatting | bytes 4194304

commit v3 on v2

--- a/solution.py
+++ b/solution.py
@@ -9,11 +9,16 @@
 STEPS = 3
 BANDS = 8
 PARTNERS = 64
-STRIDE = 27
 SLOTS = 2
 PIECE = 40
+VL = 44
 PAD = 8
 EDGE = 2
+OFFSETS = sorted(
+    ((z, x, y) for z in range(4) for x in range(4) for y in range(4)),
+    key=lambda o: (sum(d > 0 for d in o), (5 * o[0] + 11 * o[1] + 7 * o[2]) % 13),
+)
+LINES, PLANES = 10, 37
 
 
 def roll(x, amount):
@@ -22,11 +27,11 @@
 
 
 def kernel(
-    state, blocks, tile_at, row_at, kappa, lon_speed, lat_speed, mask, out,
+    state, blocks, tile_at, row_at, kappa, lon_speed, lat_speed, mask, part,
     tile_ref, row_ref, held, table, table_s, plan, send, relay, recv,
     raw_state, raw_diff, raw_zonal, raw_merid, raw_wet, raw_force, scaled,
-    q0, q1, q2, part, force, diff, zonal, merid, wet, lon_out, lon_in, lat_out, lat_in,
-    load_sem, table_sem, core_send, core_recv, send_sem, recv_sem, halo_send, halo_recv, out_sem,
+    q0, q1, q2, force, diff, zonal, merid, wet, lon_out, lon_in, lat_out, lat_in,
+    load_sem, table_sem, line_sem, core_send, core_recv, send_sem, recv_sem, halo_send, halo_recv,
 ):
     levels, rows, columns = kappa.shape
     fields = state.shape[0]
@@ -34,12 +39,16 @@
     used = SLOTS * fields + 1
     lon, lat = lax.axis_index("lon"), lax.axis_index("lat")
     core = lat % 2
-    me = lon * 2 + lat // 2
+    z, x, y = lon // 8, (lat // 2) * 2 + (lon // 4) % 2, lon % 4
     other = (lon, lat + 1 - 2 * core)
 
+    def place(i):
+        dz, dx, dy = OFFSETS[i]
+        return (z + dz) % 4, (x + dx) % 4, (y + dy) % 4
+
     def partner(i):
-        target = (me + i * STRIDE) % PARTNERS
-        return (target // 2, (target % 2) * 2 + core)
+        z, x, y = place(i)
+        return (z * 8 + (x % 2) * 4 + y, (x // 2) * 2 + core)
 
     moves = (
         (tile_at, tile_ref), (row_at, row_ref), (blocks, held), (state, raw_state.at[pl.ds(0, fields)]),
@@ -51,14 +60,8 @@
         copy.start()
 
     barrier = pltpu.get_barrier_semaphore()
-    for device in (other, (lon, 3 - lat)):
+    for device in [partner(i) for i in range(1, LINES)] + [other, (lon, 3 - lat)]:
         pl.semaphore_signal(barrier, inc=1, device_id=device, device_id_type=MESH)
-
-    def greet(i, carry):
-        pl.semaphore_signal(barrier, inc=1, device_id=partner(i), device_id_type=MESH)
-        return carry
-
-    lax.fori_loop(1, PARTNERS, greet, 0)
     loads[0].wait()
     loads[1].wait()
 
@@ -80,37 +83,43 @@
     loads[2].wait()
     to_scalars.wait()
 
-    def pack(i, carry):
-        target = (me + i * STRIDE) % PARTNERS
+    for i in range(PARTNERS):
+        tz, tx, ty = place(i)
         for h in range(2):
-            tile = (target // 2) * 4 + (target % 2) * 2 + (core if h == 0 else 1 - core)
+            tile = tz * 32 + (tx % 2) * 16 + ty * 4 + (tx // 2) * 2 + (core if h == 0 else 1 - core)
             for s in range(SLOTS):
                 send[h, i, pl.ds(s * fields, fields)] = held[table_s[s, tile]]
             send[h, i, pl.ds(SLOTS * fields, 1)] = plan[pl.ds(tile, 1), :]
-        return carry
-
-    lax.fori_loop(0, PARTNERS, pack, 0)
-
-    pl.semaphore_wait(barrier, PARTNERS + 1)
+
     across = pltpu.make_async_remote_copy(
         src_ref=send.at[1, :, pl.ds(0, used)], dst_ref=relay.at[:, pl.ds(0, used)],
         send_sem=core_send, recv_sem=core_recv, device_id=other, device_id_type=MESH,
     )
-    across.start()
-
-    def post(h):
-        def one(i, carry):
+
+    def post(h, numbers):
+        for i in numbers:
             src = send.at[0, i] if h == 0 else relay.at[i]
             pltpu.make_async_remote_copy(
                 src_ref=src.at[pl.ds(0, used)], dst_ref=recv.at[h * PARTNERS + i, pl.ds(0, used)],
                 send_sem=send_sem.at[h], recv_sem=recv_sem.at[h], device_id=partner(i), device_id_type=MESH,
             ).start()
-            return carry
-
-        lax.fori_loop(1, PARTNERS, one, 0)
-
-    post(0)
+
+    pl.semaphore_wait(barrier, LINES + 1)
+    for i in range(1, LINES):
+        pl.semaphore_signal(line_sem.at[0], inc=1, device_id=partner(i), device_id_type=MESH)
+    across.start()
+    post(0, range(1, LINES))
     recv[0] = send[0, 0]
+    pl.semaphore_wait(line_sem.at[0], LINES - 1)
+    for i in range(1, LINES):
+        pl.semaphore_signal(line_sem.at[1], inc=1, device_id=partner(i), device_id_type=MESH)
+    post(0, range(LINES, PLANES))
+    across.wait()
+    recv[PARTNERS] = relay[0]
+    post(1, range(1, PLANES))
+    pl.semaphore_wait(line_sem.at[1], LINES - 1)
+    post(0, range(PLANES, PARTNERS))
+    post(1, range(PLANES, PARTNERS))
 
     def turned(ref, r):
         flat = ref.reshape(ref.shape[0] * rows, columns)
@@ -138,9 +147,6 @@
         q0[r + EDGE, inner] = turned(raw_state, r)
 
     sweep(depth, 4, turn_state)
-    across.wait()
-    recv[PARTNERS] = relay[0]
-    post(1)
 
     east, west = ((lon + 1) % 32, lat), ((lon + 31) % 32, lat)
     lanes = lax.broadcasted_iota(jnp.int32, (8, 128), 1)
@@ -162,6 +168,12 @@
         )
 
     def start_halos(q, step):
+        to_east, to_west, to_north, to_south = halo_copies(step)
+        for r in range(depth):
+            lon_out[step, 0, pl.ds(EDGE * r, EDGE)] = q[EDGE + r, pl.ds(PAD + columns - EDGE, EDGE)]
+            lon_out[step, 1, pl.ds(EDGE * r, EDGE)] = q[EDGE + r, pl.ds(PAD, EDGE)]
+        to_east.start()
+        to_west.start()
         for k in range(EDGE):
             for half in range(2):
                 up, down = jnp.zeros((8, 128), jnp.float32), jnp.zeros((8, 128), jnp.float32)
@@ -174,12 +186,6 @@
                     down = jnp.where(lanes // width == g, roll(bottom, width * g), down)
                 lat_out[step, 0, pl.ds(8 * (2 * k + half), 8)] = up
                 lat_out[step, 1, pl.ds(8 * (2 * k + half), 8)] = down
-        for r in range(depth):
-            lon_out[step, 0, pl.ds(EDGE * r, EDGE)] = q[EDGE + r, pl.ds(PAD + columns - EDGE, EDGE)]
-            lon_out[step, 1, pl.ds(EDGE * r, EDGE)] = q[EDGE + r, pl.ds(PAD, EDGE)]
-        to_east, to_west, to_north, to_south = halo_copies(step)
-        to_east.start()
-        to_west.start()
 
         @pl.when(lat < 3)
         def _():
@@ -331,24 +337,37 @@
 
     sweep(depth - 2 * EDGE, 2, third_inside)
     wait_halos(q2, 2)
-    result = raw_state.reshape(raw_state.shape[0] * rows, columns)
-
-    def finish(r, spans):
-        for start, size in spans:
+
+    def third_ends(r):
+        for start, size in ends:
+            part[r + EDGE, pl.ds(start, size)] = advance(q2, r + EDGE, start, size)
+
+    sweep(depth - 2 * EDGE, 4, third_ends)
+    for r in (0, 1, depth - 2, depth - 1):
+        for start, size in whole:
             part[r, pl.ds(start, size)] = advance(q2, r, start, size)
-        back = jnp.transpose(part[r])
-        for b in range(BANDS):
-            result[pl.ds(b * depth + r, fields, stride=rows), :] = back[b * fields : (b + 1) * fields]
-
-    sweep(depth - 2 * EDGE, 4, lambda r: finish(r + EDGE, ends))
-    for r in (0, 1, depth - 2, depth - 1):
-        finish(r, whole)
-    store = pltpu.make_async_copy(raw_state.at[pl.ds(0, fields)], out, out_sem)
-    store.start()
     for h in range(2):
         a = recv.at[pl.ds(h * PARTNERS + 1, PARTNERS - 1), pl.ds(0, used)]
         pltpu.make_async_copy(a, a, send_sem.at[h]).wait()
-    store.wait()
+
+
+def turn_back(bands, out, result, out_sem):
+    fields, _, depth, columns = out.shape
+    flat = result.reshape((fields + 1) * BANDS * depth, columns)
+    copies = []
+    for group in range(depth // 8):
+        for r in range(group * 8, group * 8 + 8):
+            back = jnp.transpose(bands[r])
+            for b in range(BANDS):
+                flat[pl.ds(b * depth + r, fields, stride=BANDS * depth), :] = back[b * fields : (b + 1) * fields]
+        rows = pl.ds(group * 8, 8)
+        copy = pltpu.make_async_copy(
+            result.at[pl.ds(0, fields), :, rows], out.at[:, :, rows], out_sem.at[group]
+        )
+        copy.start()
+        copies.append(copy)
+    for copy in copies:
+        copy.wait()
 
 
 def body(state, blocks, dest_tile, dest_row, kappa, lon_speed, lat_speed, sea_mask):
@@ -361,29 +380,40 @@
     tall = vmem((depth + 2 * EDGE, columns + 2 * PAD, 128), f32)
     turned = vmem((depth, columns, 128), f32)
     raw, coarse = vmem((fields + 1, rows, columns), f32), vmem((levels + 1, rows, columns), f32)
-    result = pl.pallas_call(
+    bands = pl.pallas_call(
         kernel,
-        out_shape=jax.ShapeDtypeStruct(flat, f32),
+        out_shape=jax.ShapeDtypeStruct((depth, columns, 128), f32),
         in_specs=[anywhere] * 8,
-        out_specs=anywhere,
+        out_specs=pl.BlockSpec(memory_space=pltpu.VMEM),
         scratch_shapes=[
             vmem((1, 128), i32), vmem((1, 128), i32), vmem((128, fields, columns), f32),
             vmem((8, 128), i32), pltpu.SMEM((8, 128), i32), vmem((128, 128), f32),
             vmem((2, PARTNERS, PIECE, columns), f32), vmem((PARTNERS, PIECE, columns), f32),
             vmem((2 * PARTNERS + 1, PIECE, columns), f32),
             raw, coarse, coarse, coarse, vmem((levels, rows, columns), i32), raw, coarse,
-            tall, tall, tall, turned, turned, turned, turned, turned, turned,
+            tall, tall, tall, turned, turned, turned, turned, turned,
             vmem((STEPS, 2, EDGE * depth, 128), f32), vmem((STEPS, 2, EDGE * depth, 128), f32),
             vmem((STEPS, 2, 16 * EDGE, 128), f32), vmem((STEPS, 2, 16 * EDGE, 128), f32),
-            dma((8,)), dma, dma, dma, dma((2,)), dma((2,)), dma((STEPS, 4)), dma((STEPS, 4)), dma,
+            dma((8,)), dma, pltpu.SemaphoreType.REGULAR((2,)), dma, dma, dma((2,)), dma((2,)), dma((STEPS, 4)), dma((STEPS, 4)),
         ],
         compiler_params=pltpu.CompilerParams(
-            collective_id=0, has_side_effects=True, vmem_limit_bytes=63 << 20
+            collective_id=0, has_side_effects=True, vmem_limit_bytes=VL << 20
         ),
-    )(
-        state.reshape(flat), blocks.reshape(128, fields, columns), dest_tile.reshape(1, 128), dest_row.reshape(1, 128),
-        kappa, lon_speed, lat_speed, sea_mask,
-    )
+    )(*[
+        pltpu.with_memory_space_constraint(x, pltpu.HBM)
+        for x in (
+            state.reshape(flat), blocks.reshape(128, fields, columns), dest_tile.reshape(1, 128),
+            dest_row.reshape(1, 128), kappa, lon_speed, lat_speed, sea_mask,
+        )
+    ])
+    result = pl.pallas_call(
+        turn_back,
+        out_shape=jax.ShapeDtypeStruct((fields, BANDS, depth, columns), f32),
+        in_specs=[pl.BlockSpec(memory_space=pltpu.VMEM)],
+        out_specs=anywhere,
+        scratch_shapes=[vmem((fields + 1, BANDS, depth, columns), f32), dma((depth // 8,))],
+        compiler_params=pltpu.CompilerParams(vmem_limit_bytes=16 << 20),
+    )(bands)
     return result.reshape(state.shape)
 
 

time: 60.8 us -> 55.5 us (0.913); the launches traced: 60.7 us -> 54.7 us
  local copies, waits for them, and re-layouts: 3.11 us -> 0 us
  Pallas kernels: 57.6 us -> 54.7 us
    unnamed x1 -> x0, local copies, waits for them, and re-layouts: 3.11 us -> none
    pallas_call x1 -> x2, Pallas kernels: 57.6 us -> 54.7 us  [the longest x1 52.3 us: body(): pl.pallas_call(kernel, out_shape=jax.ShapeDtypeStruct((depth, columns, 12...]
where the time goes in v3:
time: 55.5 us; the launch traced here: 54.7 us
  Pallas kernels  54.7 us (99%)
    pallas_call x1, Pallas kernels, body(): pl.pallas_call(kernel, out_shape=jax.ShapeDtypeStruct((depth, columns, 12...  52.3 us
    pallas_call x1, Pallas kernels, body(): pl.pallas_call(turn_back, out_shape=jax.ShapeDtypeStruct((fields, BANDS,...  2.37 us

profile of v3, /device:TPU:1, one launch (start us, length us, event | category | flops | bytes accessed | tf_op | source)
XLA Modules:
  0.0 54.7 jit_solution(14107472753570423218)
XLA Ops:
  0.0 52.3 %shard_map.82.bands = f32[32,128,128]{2,1,0:T(8,128)S(1)} custom-call(f32[16,256,128]{2,1,0:T(8,128)} %bitcast.5, f32[128,16,128]{2,1,0:T(8,128)} %bitcast.6, s32[1,128]{1,0:T(1,128)} %bitcast.7, s32[1,128]{1,0:T(1,128)} %bitcast.8, f32[8,256,128]{2,1,0:T(8,128)} %kappa.1, f32[8,256,128]{2,1,0:T(8,128)} %lon_speed.1, f32[8,256,128]{2,1,0:T(8,128)} %lat_speed.1, ...), custom_call_target="tpu_custom_call" | custom-call | tf_op jit(solution)/shard_map/pallas_call | solution.py:383
  52.3 2.4 %shard_map.83 = f32[16,8,32,128]{3,2,1,0:T(8,128)} custom-call(f32[32,128,128]{2,1,0:T(8,128)S(1)} %shard_map.82.bands), custom_call_target="tpu_custom_call" | custom-call | tf_op jit(solution)/shard_map/pallas_call | solution.py:409

commit v4 on v3

--- a/solution.py
+++ b/solution.py
@@ -16,7 +16,7 @@
 EDGE = 2
 OFFSETS = sorted(
     ((z, x, y) for z in range(4) for x in range(4) for y in range(4)),
-    key=lambda o: (sum(d > 0 for d in o), (5 * o[0] + 11 * o[1] + 7 * o[2]) % 13),
+    key=lambda o: (sum(d > 0 for d in o), -sum(d == 2 for d in o), (5 * o[0] + 11 * o[1] + 7 * o[2]) % 13),
 )
 LINES, PLANES = 10, 37
 
@@ -56,11 +56,12 @@
         (lat_speed, raw_merid.at[pl.ds(0, levels)]), (mask, raw_wet),
     )
     loads = [pltpu.make_async_copy(src, dst, load_sem.at[k]) for k, (src, dst) in enumerate(moves)]
-    for copy in loads:
+    for copy in loads[:4]:
         copy.start()
+    east, west = ((lon + 1) % 32, lat), ((lon + 31) % 32, lat)
 
     barrier = pltpu.get_barrier_semaphore()
-    for device in [partner(i) for i in range(1, LINES)] + [other, (lon, 3 - lat)]:
+    for device in [partner(i) for i in range(1, LINES)] + [other, (lon, 3 - lat), east, west]:
         pl.semaphore_signal(barrier, inc=1, device_id=device, device_id_type=MESH)
     loads[0].wait()
     loads[1].wait()
@@ -83,54 +84,22 @@
     loads[2].wait()
     to_scalars.wait()
 
-    for i in range(PARTNERS):
-        tz, tx, ty = place(i)
-        for h in range(2):
+    def pack(h, numbers):
+        for i in numbers:
+            tz, tx, ty = place(i)
             tile = tz * 32 + (tx % 2) * 16 + ty * 4 + (tx // 2) * 2 + (core if h == 0 else 1 - core)
             for s in range(SLOTS):
                 send[h, i, pl.ds(s * fields, fields)] = held[table_s[s, tile]]
             send[h, i, pl.ds(SLOTS * fields, 1)] = plan[pl.ds(tile, 1), :]
 
-    across = pltpu.make_async_remote_copy(
-        src_ref=send.at[1, :, pl.ds(0, used)], dst_ref=relay.at[:, pl.ds(0, used)],
-        send_sem=core_send, recv_sem=core_recv, device_id=other, device_id_type=MESH,
-    )
-
-    def post(h, numbers):
-        for i in numbers:
-            src = send.at[0, i] if h == 0 else relay.at[i]
-            pltpu.make_async_remote_copy(
-                src_ref=src.at[pl.ds(0, used)], dst_ref=recv.at[h * PARTNERS + i, pl.ds(0, used)],
-                send_sem=send_sem.at[h], recv_sem=recv_sem.at[h], device_id=partner(i), device_id_type=MESH,
-            ).start()
-
-    pl.semaphore_wait(barrier, LINES + 1)
-    for i in range(1, LINES):
-        pl.semaphore_signal(line_sem.at[0], inc=1, device_id=partner(i), device_id_type=MESH)
-    across.start()
-    post(0, range(1, LINES))
-    recv[0] = send[0, 0]
-    pl.semaphore_wait(line_sem.at[0], LINES - 1)
-    for i in range(1, LINES):
-        pl.semaphore_signal(line_sem.at[1], inc=1, device_id=partner(i), device_id_type=MESH)
-    post(0, range(LINES, PLANES))
-    across.wait()
-    recv[PARTNERS] = relay[0]
-    post(1, range(1, PLANES))
-    pl.semaphore_wait(line_sem.at[1], LINES - 1)
-    post(0, range(PLANES, PARTNERS))
-    post(1, range(PLANES, PARTNERS))
+    pack(1, range(PARTNERS))
+    pack(0, range(PARTNERS))
 
     def turned(ref, r):
         flat = ref.reshape(ref.shape[0] * rows, columns)
-        taken = []
-        for b in range(BANDS):
-            if ref.shape[0] > fields:
-                taken.append(flat[pl.ds(b * depth + r, fields, stride=rows), :])
-            else:
-                level = flat[pl.ds(b * depth + r, levels, stride=rows), :]
-                taken += [level] * (fields // levels)
-        return jnp.transpose(jnp.concatenate(taken, axis=0))
+        count = ref.shape[0] - 1
+        taken = [flat[pl.ds(n * rows + r, BANDS, stride=depth), :] for n in range(count)]
+        return jnp.transpose(jnp.concatenate(taken * (fields // count), axis=0))
 
     def sweep(count, unroll, step):
         def some(i, carry):
@@ -141,17 +110,8 @@
         lax.fori_loop(0, count // unroll, some, 0)
 
     inner = pl.ds(PAD, columns)
-    loads[3].wait()
-
-    def turn_state(r):
-        q0[r + EDGE, inner] = turned(raw_state, r)
-
-    sweep(depth, 4, turn_state)
-
-    east, west = ((lon + 1) % 32, lat), ((lon + 31) % 32, lat)
+
     lanes = lax.broadcasted_iota(jnp.int32, (8, 128), 1)
-    width = 128 // BANDS
-    many = columns // 8
 
     def halo_copies(step):
         def copy(src, dst, k, device):
@@ -167,25 +127,31 @@
             copy(lat_out.at[step, 1], lat_in.at[step, 1], 3, (lon, jnp.maximum(lat - 1, 0))),
         )
 
-    def start_halos(q, step):
+    def start_halos(q, step, now=True):
         to_east, to_west, to_north, to_south = halo_copies(step)
         for r in range(depth):
             lon_out[step, 0, pl.ds(EDGE * r, EDGE)] = q[EDGE + r, pl.ds(PAD + columns - EDGE, EDGE)]
             lon_out[step, 1, pl.ds(EDGE * r, EDGE)] = q[EDGE + r, pl.ds(PAD, EDGE)]
-        to_east.start()
-        to_west.start()
+        if now:
+            to_east.start()
+            to_west.start()
         for k in range(EDGE):
             for half in range(2):
                 up, down = jnp.zeros((8, 128), jnp.float32), jnp.zeros((8, 128), jnp.float32)
                 for g in range(BANDS):
                     at = pl.ds(PAD + 8 * (half * BANDS + g), 8)
                     top, bottom = q[depth + k, at], q[EDGE + k, at]
-                    q[k, at] = roll(top, width)
-                    q[EDGE + depth + k, at] = roll(bottom, -width)
-                    up = jnp.where(lanes // width == g, roll(top, width * (g + 1)), up)
-                    down = jnp.where(lanes // width == g, roll(bottom, width * g), down)
+                    q[k, at] = roll(top, 1)
+                    q[EDGE + depth + k, at] = roll(bottom, -1)
+                    up = jnp.where(lanes % BANDS == g, roll(top, g + 1 - BANDS), up)
+                    down = jnp.where(lanes % BANDS == g, roll(bottom, g), down)
                 lat_out[step, 0, pl.ds(8 * (2 * k + half), 8)] = up
                 lat_out[step, 1, pl.ds(8 * (2 * k + half), 8)] = down
+        if now:
+            send_lat_halos(step)
+
+    def send_lat_halos(step):
+        _, _, to_north, to_south = halo_copies(step)
 
         @pl.when(lat < 3)
         def _():
@@ -194,20 +160,24 @@
         @pl.when(lat > 0)
         def _():
             to_south.start()
+
+    def send_halos(step):
+        to_east, to_west, _, _ = halo_copies(step)
+        to_east.start()
+        to_west.start()
+        send_lat_halos(step)
 
     def wait_halos(q, step):
         to_east, to_west, to_north, to_south = halo_copies(step)
-        to_east.wait()
-        to_west.wait()
+        to_east.wait_recv()
+        to_west.wait_recv()
 
         @pl.when(lat < 3)
         def _():
-            to_north.wait_send()
             to_south.wait_recv()
 
         @pl.when(lat > 0)
         def _():
-            to_south.wait_send()
             to_north.wait_recv()
 
         for r in range(depth):
@@ -219,9 +189,9 @@
                 above = lat_in[step, 1, pl.ds(8 * (2 * k + half), 8)]
                 for g in range(BANDS):
                     at = pl.ds(PAD + 8 * (half * BANDS + g), 8)
-                    q[k, at] = jnp.where(lanes < width, roll(below, -width * g), q[k, at])
+                    q[k, at] = jnp.where(lanes % BANDS == 0, roll(below, -g), q[k, at])
                     n = EDGE + depth + k
-                    q[n, at] = jnp.where(lanes >= 128 - width, roll(above, -width * (g + 1)), q[n, at])
+                    q[n, at] = jnp.where(lanes % BANDS == BANDS - 1, roll(above, BANDS - 1 - g), q[n, at])
 
     blank = jnp.zeros(lat_in.shape[2:], jnp.float32)
     for step in range(STEPS):
@@ -234,7 +204,48 @@
         def _():
             lat_in[step, 1] = blank
 
+
+    across = pltpu.make_async_remote_copy(
+        src_ref=send.at[1, :, pl.ds(0, used)], dst_ref=relay.at[:, pl.ds(0, used)],
+        send_sem=core_send, recv_sem=core_recv, device_id=other, device_id_type=MESH,
+    )
+
+    def post(h, numbers):
+        for i in numbers:
+            src = send.at[0, i] if h == 0 else relay.at[i]
+            pltpu.make_async_remote_copy(
+                src_ref=src.at[pl.ds(0, used)], dst_ref=recv.at[h * PARTNERS + i, pl.ds(0, used)],
+                send_sem=send_sem.at[h], recv_sem=recv_sem.at[h], device_id=partner(i), device_id_type=MESH,
+            ).start()
+
+    pl.semaphore_wait(barrier, LINES + 3)
+    for i in range(1, LINES):
+        pl.semaphore_signal(line_sem.at[0], inc=1, device_id=partner(i), device_id_type=MESH)
+    across.start()
+    post(0, range(1, LINES))
+    for copy in loads[4:]:
+        copy.start()
+    recv[0] = send[0, 0]
+
+    loads[3].wait()
+
+    def turn_state(r):
+        q0[r + EDGE, inner] = turned(raw_state, r)
+
+    sweep(depth, 4, turn_state)
+
     start_halos(q0, 0)
+    pl.semaphore_wait(line_sem.at[0], LINES - 1)
+    for i in range(1, LINES):
+        pl.semaphore_signal(line_sem.at[1], inc=1, device_id=partner(i), device_id_type=MESH)
+    post(0, range(LINES, PLANES))
+    pl.semaphore_wait(line_sem.at[1], LINES - 1)
+    post(0, range(PLANES, PARTNERS))
+    across.wait_recv()
+    recv[PARTNERS] = relay[0]
+    for numbers in (range(PLANES, PARTNERS), range(LINES, PLANES), range(1, LINES)):
+        post(1, numbers)
+
 
     for copy in loads[4:]:
         copy.wait()
@@ -282,27 +293,35 @@
 
     sweep(depth, 2, first_step)
 
+    place_row = lax.broadcasted_iota(jnp.int32, (rows, 128), 0)
+    grid_row = (place_row % BANDS * depth + place_row // BANDS).astype(jnp.float32)
+    slot_lane = lax.broadcasted_iota(jnp.int32, (1, 128), 1)
+    flat = recv.reshape(recv.shape[0] * PIECE, columns)
+
     for h in range(2):
         a = recv.at[pl.ds(h * PARTNERS + 1, PARTNERS - 1), pl.ds(0, used)]
         pltpu.make_async_copy(a, a, recv_sem.at[h]).wait()
-    flat = recv.reshape(recv.shape[0] * PIECE, columns)
-    rows_of = jnp.transpose(flat[pl.ds(SLOTS * fields, 128, stride=PIECE), :])
-    grid_row = lax.broadcasted_iota(jnp.int32, (rows, 128), 0).astype(jnp.float32)
-    selector = jnp.concatenate(
-        [jnp.where(grid_row == rows_of[s : s + 1], 1.0, 0.0).astype(jnp.bfloat16) for s in range(SLOTS)], axis=1
-    )
-
-    def assemble(n):
-        data = jnp.concatenate([flat[pl.ds(s * fields + n, 128, stride=PIECE), :] for s in range(SLOTS)], axis=0)
-        high = data.astype(jnp.bfloat16)
-        rest = (data - high.astype(jnp.float32)).astype(jnp.bfloat16)
-        both = jnp.dot(selector, jnp.concatenate([high, rest], axis=1), preferred_element_type=jnp.float32)
-        raw_force[n] = both[:, :columns] + both[:, columns:]
-
-    sweep(fields, 2, assemble)
+
+        def taken(n):
+            return flat[pl.ds(h * PARTNERS * PIECE + n, PARTNERS, stride=PIECE), :]
+
+        named_rows = taken(SLOTS * fields)
+        rows_of = jnp.transpose(jnp.concatenate([named_rows] * SLOTS, axis=0))
+        rows_of = jnp.where(slot_lane < PARTNERS, rows_of[0:1], rows_of[1:2])
+        selector = jnp.where(grid_row == rows_of, 1.0, 0.0).astype(jnp.bfloat16)
+
+        def assemble(n):
+            data = jnp.concatenate([taken(s * fields + n) for s in range(SLOTS)], axis=0)
+            high = data.astype(jnp.bfloat16)
+            rest = (data - high.astype(jnp.float32)).astype(jnp.bfloat16)
+            both = jnp.dot(selector, jnp.concatenate([high, rest], axis=1), preferred_element_type=jnp.float32)
+            total = (both[:, :columns] + both[:, columns:]).reshape(depth, BANDS, columns)
+            raw_force[n] = total if h == 0 else raw_force[n] + total
+
+        sweep(fields, 8, assemble)
 
     def add_forcing(r):
-        forcing = turned(raw_force, r) * wet[r]
+        forcing = jnp.transpose(raw_force[:, r].reshape(fields * BANDS, columns)) * wet[r]
         force[r] = forcing
         q1[r + EDGE, inner] = part[r] + forcing
 
@@ -346,6 +365,20 @@
     for r in (0, 1, depth - 2, depth - 1):
         for start, size in whole:
             part[r, pl.ds(start, size)] = advance(q2, r, start, size)
+    for step in range(STEPS):
+        to_east, to_west, to_north, to_south = halo_copies(step)
+        to_east.wait_send()
+        to_west.wait_send()
+
+        @pl.when(lat < 3)
+        def _():
+            to_north.wait_send()
+
+        @pl.when(lat > 0)
+        def _():
+            to_south.wait_send()
+
+    across.wait_send()
     for h in range(2):
         a = recv.at[pl.ds(h * PARTNERS + 1, PARTNERS - 1), pl.ds(0, used)]
         pltpu.make_async_copy(a, a, send_sem.at[h]).wait()
@@ -358,8 +391,8 @@
     for group in range(depth // 8):
         for r in range(group * 8, group * 8 + 8):
             back = jnp.transpose(bands[r])
-            for b in range(BANDS):
-                flat[pl.ds(b * depth + r, fields, stride=BANDS * depth), :] = back[b * fields : (b + 1) * fields]
+            for n in range(fields):
+                flat[pl.ds(n * BANDS * depth + r, BANDS, stride=depth), :] = back[n * BANDS : (n + 1) * BANDS]
         rows = pl.ds(group * 8, 8)
         copy = pltpu.make_async_copy(
             result.at[pl.ds(0, fields), :, rows], out.at[:, :, rows], out_sem.at[group]
@@ -390,7 +423,8 @@
             vmem((8, 128), i32), pltpu.SMEM((8, 128), i32), vmem((128, 128), f32),
             vmem((2, PARTNERS, PIECE, columns), f32), vmem((PARTNERS, PIECE, columns), f32),
             vmem((2 * PARTNERS + 1, PIECE, columns), f32),
-            raw, coarse, coarse, coarse, vmem((levels, rows, columns), i32), raw, coarse,
+            raw, coarse, coarse, coarse, vmem((levels, rows, columns), i32),
+            vmem((fields, depth, BANDS, columns), f32), coarse,
             tall, tall, tall, turned, turned, turned, turned, turned,
             vmem((STEPS, 2, EDGE * depth, 128), f32), vmem((STEPS, 2, EDGE * depth, 128), f32),
             vmem((STEPS, 2, 16 * EDGE, 128), f32), vmem((STEPS, 2, 16 * EDGE, 128), f32),

time: 55.5 us -> 51.8 us (0.933)
  Pallas kernels: 54.7 us -> 50.8 us
    pallas_call x1, Pallas kernels: 52.3 us -> 48.5 us  [body(): pl.pallas_call(kernel, out_shape=jax.ShapeDtypeStruct((depth, columns, 12...]
where the time goes in v4:
time: 51.8 us; the launch traced here: 50.9 us
  Pallas kernels  50.8 us (98%)
    pallas_call x1, Pallas kernels, body(): pl.pallas_call(kernel, out_shape=jax.ShapeDtypeStruct((depth, columns, 12...  48.5 us
    pallas_call x1, Pallas kernels, body(): pl.pallas_call(turn_back, out_shape=jax.ShapeDtypeStruct((fields, BANDS,...  2.36 us

profile of v4, /device:TPU:1, one launch (start us, length us, event | category | flops | bytes accessed | tf_op | source)
XLA Modules:
  0.0 50.9 jit_solution(2719795271043042181)
XLA Ops:
  0.0 48.5 %shard_map.82.bands = f32[32,128,128]{2,1,0:T(8,128)S(1)} custom-call(f32[16,256,128]{2,1,0:T(8,128)} %bitcast.5, f32[128,16,128]{2,1,0:T(8,128)} %bitcast.6, s32[1,128]{1,0:T(1,128)} %bitcast.7, s32[1,128]{1,0:T(1,128)} %bitcast.8, f32[8,256,128]{2,1,0:T(8,128)} %kappa.1, f32[8,256,128]{2,1,0:T(8,128)} %lon_speed.1, f32[8,256,128]{2,1,0:T(8,128)} %lat_speed.1, ...), custom_call_target="tpu_custom_call" | custom-call | tf_op jit(solution)/shard_map/pallas_call | solution.py:416
  48.5 2.4 %shard_map.83 = f32[16,8,32,128]{3,2,1,0:T(8,128)} custom-call(f32[32,128,128]{2,1,0:T(8,128)S(1)} %shard_map.82.bands), custom_call_target="tpu_custom_call" | custom-call | tf_op jit(solution)/shard_map/pallas_call | solution.py:443

commit v5 on v4

--- a/solution.py
+++ b/solution.py
@@ -16,7 +16,7 @@
 EDGE = 2
 OFFSETS = sorted(
     ((z, x, y) for z in range(4) for x in range(4) for y in range(4)),
-    key=lambda o: (sum(d > 0 for d in o), -sum(d == 2 for d in o), (5 * o[0] + 11 * o[1] + 7 * o[2]) % 13),
+    key=lambda o: (sum(d > 0 for d in o), -sum(d == 2 for d in o), (16 * o[0] + 4 * o[1] + o[2]) * 27 % 64),
 )
 LINES, PLANES = 10, 37
 
@@ -36,7 +36,7 @@
     levels, rows, columns = kappa.shape
     fields = state.shape[0]
     depth = rows // BANDS
-    used = SLOTS * fields + 1
+    used = (SLOTS * fields, SLOTS * fields + 1)
     lon, lat = lax.axis_index("lon"), lax.axis_index("lat")
     core = lat % 2
     z, x, y = lon // 8, (lat // 2) * 2 + (lon // 4) % 2, lon % 4
@@ -76,7 +76,7 @@
     last_row = jnp.sum(jnp.where(number == last, row_f, 0.0), axis=1, keepdims=True)
     first_row = jnp.where(last >= 0, first_row, -1.0)
     last_row = jnp.where(last > first, last_row, -1.0)
-    plan[...] = jnp.where(number == 0, first_row, last_row)
+    plan[...] = jnp.where(number % SLOTS == 0, first_row, last_row)
     slots = jnp.where(number == 0, jnp.minimum(first, 127), jnp.maximum(last, 0))
     table[...] = jnp.transpose(slots)[:8]
     to_scalars = pltpu.make_async_copy(table, table_s, table_sem)
@@ -84,13 +84,16 @@
     loads[2].wait()
     to_scalars.wait()
 
+    def tile(h, i):
+        tz, tx, ty = place(i)
+        return tz * 32 + (tx % 2) * 16 + ty * 4 + (tx // 2) * 2 + (core if h == 0 else 1 - core)
+
     def pack(h, numbers):
         for i in numbers:
-            tz, tx, ty = place(i)
-            tile = tz * 32 + (tx % 2) * 16 + ty * 4 + (tx // 2) * 2 + (core if h == 0 else 1 - core)
             for s in range(SLOTS):
-                send[h, i, pl.ds(s * fields, fields)] = held[table_s[s, tile]]
-            send[h, i, pl.ds(SLOTS * fields, 1)] = plan[pl.ds(tile, 1), :]
+                send[h, i, pl.ds(s * fields, fields)] = held[table_s[s, tile(h, i)]]
+            if h == 1:
+                send[h, i, pl.ds(SLOTS * fields, 1)] = plan[pl.ds(tile(h, i), 1), :]
 
     pack(1, range(PARTNERS))
     pack(0, range(PARTNERS))
@@ -113,28 +116,35 @@
 
     lanes = lax.broadcasted_iota(jnp.int32, (8, 128), 1)
 
-    def halo_copies(step):
-        def copy(src, dst, k, device):
-            return pltpu.make_async_remote_copy(
-                src_ref=src, dst_ref=dst, send_sem=halo_send.at[step, k], recv_sem=halo_recv.at[step, k],
-                device_id=device, device_id_type=MESH,
-            )
-
-        return (
-            copy(lon_out.at[step, 0], lon_in.at[step, 0], 0, east),
-            copy(lon_out.at[step, 1], lon_in.at[step, 1], 1, west),
-            copy(lat_out.at[step, 0], lat_in.at[step, 0], 2, (lon, jnp.minimum(lat + 1, 3))),
-            copy(lat_out.at[step, 1], lat_in.at[step, 1], 3, (lon, jnp.maximum(lat - 1, 0))),
+    def halo_copy(src, dst, step, k, device):
+        return pltpu.make_async_remote_copy(
+            src_ref=src, dst_ref=dst, send_sem=halo_send.at[step, k], recv_sem=halo_recv.at[step, k],
+            device_id=device, device_id_type=MESH,
         )
 
-    def start_halos(q, step, now=True):
-        to_east, to_west, to_north, to_south = halo_copies(step)
-        for r in range(depth):
-            lon_out[step, 0, pl.ds(EDGE * r, EDGE)] = q[EDGE + r, pl.ds(PAD + columns - EDGE, EDGE)]
-            lon_out[step, 1, pl.ds(EDGE * r, EDGE)] = q[EDGE + r, pl.ds(PAD, EDGE)]
-        if now:
-            to_east.start()
-            to_west.start()
+    def lon_copies(step, half):
+        return [
+            halo_copy(lon_out.at[step, d, half], lon_in.at[step, d, half], step, 2 * half + d, device)
+            for d, device in enumerate((east, west))
+        ]
+
+    def lat_copies(step):
+        return [
+            halo_copy(lat_out.at[step, d], lat_in.at[step, d], step, 4 + d, (lon, there))
+            for d, there in enumerate((jnp.minimum(lat + 1, 3), jnp.maximum(lat - 1, 0)))
+        ]
+
+    half_depth = depth // 2
+
+    def start_lon(q, step, half):
+        for k in range(half_depth):
+            n, at = EDGE + half * half_depth + k, pl.ds(EDGE * k, EDGE)
+            lon_out[step, 0, half, at] = q[n, pl.ds(PAD + columns - EDGE, EDGE)]
+            lon_out[step, 1, half, at] = q[n, pl.ds(PAD, EDGE)]
+        for copy in lon_copies(step, half):
+            copy.start()
+
+    def start_lat(q, step):
         for k in range(EDGE):
             for half in range(2):
                 up, down = jnp.zeros((8, 128), jnp.float32), jnp.zeros((8, 128), jnp.float32)
@@ -147,11 +157,7 @@
                     down = jnp.where(lanes % BANDS == g, roll(bottom, g), down)
                 lat_out[step, 0, pl.ds(8 * (2 * k + half), 8)] = up
                 lat_out[step, 1, pl.ds(8 * (2 * k + half), 8)] = down
-        if now:
-            send_lat_halos(step)
-
-    def send_lat_halos(step):
-        _, _, to_north, to_south = halo_copies(step)
+        to_north, to_south = lat_copies(step)
 
         @pl.when(lat < 3)
         def _():
@@ -161,16 +167,16 @@
         def _():
             to_south.start()
 
-    def send_halos(step):
-        to_east, to_west, _, _ = halo_copies(step)
-        to_east.start()
-        to_west.start()
-        send_lat_halos(step)
-
-    def wait_halos(q, step):
-        to_east, to_west, to_north, to_south = halo_copies(step)
-        to_east.wait_recv()
-        to_west.wait_recv()
+    def wait_lon(q, step, half):
+        for copy in lon_copies(step, half):
+            copy.wait_recv()
+        for k in range(half_depth):
+            n, at = EDGE + half * half_depth + k, pl.ds(EDGE * k, EDGE)
+            q[n, pl.ds(PAD - EDGE, EDGE)] = lon_in[step, 0, half, at]
+            q[n, pl.ds(PAD + columns, EDGE)] = lon_in[step, 1, half, at]
+
+    def wait_lat(q, step):
+        to_north, to_south = lat_copies(step)
 
         @pl.when(lat < 3)
         def _():
@@ -180,9 +186,6 @@
         def _():
             to_north.wait_recv()
 
-        for r in range(depth):
-            q[EDGE + r, pl.ds(PAD - EDGE, EDGE)] = lon_in[step, 0, pl.ds(EDGE * r, EDGE)]
-            q[EDGE + r, pl.ds(PAD + columns, EDGE)] = lon_in[step, 1, pl.ds(EDGE * r, EDGE)]
         for k in range(EDGE):
             for half in range(2):
                 below = lat_in[step, 0, pl.ds(8 * (2 * k + half), 8)]
@@ -206,15 +209,17 @@
 
 
     across = pltpu.make_async_remote_copy(
-        src_ref=send.at[1, :, pl.ds(0, used)], dst_ref=relay.at[:, pl.ds(0, used)],
+        src_ref=send.at[1, :, pl.ds(0, used[1])], dst_ref=relay.at[:, pl.ds(0, used[1])],
         send_sem=core_send, recv_sem=core_recv, device_id=other, device_id_type=MESH,
     )
+
+    slot_lane = lax.broadcasted_iota(jnp.int32, (1, 128), 1)
 
     def post(h, numbers):
         for i in numbers:
             src = send.at[0, i] if h == 0 else relay.at[i]
             pltpu.make_async_remote_copy(
-                src_ref=src.at[pl.ds(0, used)], dst_ref=recv.at[h * PARTNERS + i, pl.ds(0, used)],
+                src_ref=src.at[pl.ds(0, used[h])], dst_ref=recv.at[h * PARTNERS + i, pl.ds(0, used[h])],
                 send_sem=send_sem.at[h], recv_sem=recv_sem.at[h], device_id=partner(i), device_id_type=MESH,
             ).start()
 
@@ -234,7 +239,9 @@
 
     sweep(depth, 4, turn_state)
 
-    start_halos(q0, 0)
+    for half in range(2):
+        start_lon(q0, 0, half)
+    start_lat(q0, 0)
     pl.semaphore_wait(line_sem.at[0], LINES - 1)
     for i in range(1, LINES):
         pl.semaphore_signal(line_sem.at[1], inc=1, device_id=partner(i), device_id_type=MESH)
@@ -242,6 +249,9 @@
     pl.semaphore_wait(line_sem.at[1], LINES - 1)
     post(0, range(PLANES, PARTNERS))
     across.wait_recv()
+    for i in range(PARTNERS):
+        at = (i, pl.ds(SLOTS * fields, 1))
+        relay[at] = jnp.where(slot_lane < SLOTS, relay[at], plan[pl.ds(tile(0, i), 1), :])
     recv[PARTNERS] = relay[0]
     for numbers in (range(PLANES, PARTNERS), range(LINES, PLANES), range(1, LINES)):
         post(1, numbers)
@@ -285,7 +295,9 @@
     middle = [(8, 32), (40, 32), (72, 32), (104, 16)]
     ends = [(0, 8), (columns - 8, 8)]
 
-    wait_halos(q0, 0)
+    wait_lat(q0, 0)
+    for half in range(2):
+        wait_lon(q0, 0, half)
 
     def first_step(r):
         for start, size in whole:
@@ -293,82 +305,86 @@
 
     sweep(depth, 2, first_step)
 
+    for h in range(2):
+        a = recv.at[pl.ds(h * PARTNERS + 1, PARTNERS - 1), pl.ds(0, used[h])]
+        pltpu.make_async_copy(a, a, recv_sem.at[h]).wait()
     place_row = lax.broadcasted_iota(jnp.int32, (rows, 128), 0)
     grid_row = (place_row % BANDS * depth + place_row // BANDS).astype(jnp.float32)
-    slot_lane = lax.broadcasted_iota(jnp.int32, (1, 128), 1)
     flat = recv.reshape(recv.shape[0] * PIECE, columns)
 
+    def taken(h, n):
+        return flat[pl.ds(h * PARTNERS * PIECE + n, PARTNERS, stride=PIECE), :]
+
+    rows_of = jnp.transpose(jnp.concatenate([taken(1, SLOTS * fields)] * SLOTS, axis=0))
+    selector = []
     for h in range(2):
-        a = recv.at[pl.ds(h * PARTNERS + 1, PARTNERS - 1), pl.ds(0, used)]
-        pltpu.make_async_copy(a, a, recv_sem.at[h]).wait()
-
-        def taken(n):
-            return flat[pl.ds(h * PARTNERS * PIECE + n, PARTNERS, stride=PIECE), :]
-
-        named_rows = taken(SLOTS * fields)
-        rows_of = jnp.transpose(jnp.concatenate([named_rows] * SLOTS, axis=0))
-        rows_of = jnp.where(slot_lane < PARTNERS, rows_of[0:1], rows_of[1:2])
-        selector = jnp.where(grid_row == rows_of, 1.0, 0.0).astype(jnp.bfloat16)
-
-        def assemble(n):
-            data = jnp.concatenate([taken(s * fields + n) for s in range(SLOTS)], axis=0)
-            high = data.astype(jnp.bfloat16)
-            rest = (data - high.astype(jnp.float32)).astype(jnp.bfloat16)
-            both = jnp.dot(selector, jnp.concatenate([high, rest], axis=1), preferred_element_type=jnp.float32)
-            total = (both[:, :columns] + both[:, columns:]).reshape(depth, BANDS, columns)
-            raw_force[n] = total if h == 0 else raw_force[n] + total
-
-        sweep(fields, 8, assemble)
+        own = SLOTS * (1 - h)
+        named_rows = jnp.where(slot_lane < PARTNERS, rows_of[own : own + 1], rows_of[own + 1 : own + 2])
+        selector.append(jnp.where(grid_row == named_rows, 1.0, 0.0).astype(jnp.bfloat16))
+    selector = jnp.concatenate(selector, axis=1)
+
+    def assemble(n):
+        data = jnp.concatenate([taken(h, s * fields + n) for h in range(2) for s in range(SLOTS)], axis=0)
+        high = data.astype(jnp.bfloat16)
+        rest = (data - high.astype(jnp.float32)).astype(jnp.bfloat16)
+        both = jnp.dot(selector, jnp.concatenate([high, rest], axis=1), preferred_element_type=jnp.float32)
+        raw_force[n] = (both[:, :columns] + both[:, columns:]).reshape(depth, BANDS, columns)
+
+    sweep(fields, 8, assemble)
 
     def add_forcing(r):
         forcing = jnp.transpose(raw_force[:, r].reshape(fields * BANDS, columns)) * wet[r]
         force[r] = forcing
         q1[r + EDGE, inner] = part[r] + forcing
 
-    sweep(depth, 4, add_forcing)
+    def sweep_from(start, count, unroll, step):
+        sweep(count, unroll, lambda r: step(r + start))
+
+    for half in range(2):
+        sweep_from(half * half_depth, half_depth, 4, add_forcing)
+        start_lon(q1, 1, half)
+    start_lat(q1, 1)
 
     def advance(q, r, start, size):
         return stencil(q, r, start, size) + force[r, pl.ds(start, size)]
 
-    start_halos(q1, 1)
-
-    def second_inside(r):
-        for start, size in middle:
-            q2[r + 2 * EDGE, pl.ds(PAD + start, size)] = advance(q1, r + EDGE, start, size)
-
-    sweep(depth - 2 * EDGE, 2, second_inside)
-    wait_halos(q1, 1)
-
-    def second_ends(r):
-        for start, size in ends:
-            q2[r + 2 * EDGE, pl.ds(PAD + start, size)] = advance(q1, r + EDGE, start, size)
-
-    sweep(depth - 2 * EDGE, 4, second_ends)
-    for r in (0, 1, depth - 2, depth - 1):
-        for start, size in whole:
-            q2[r + EDGE, pl.ds(PAD + start, size)] = advance(q1, r, start, size)
-
-    start_halos(q2, 2)
-
-    def third_inside(r):
-        for start, size in middle:
-            part[r + EDGE, pl.ds(start, size)] = advance(q2, r + EDGE, start, size)
-
-    sweep(depth - 2 * EDGE, 2, third_inside)
-    wait_halos(q2, 2)
-
-    def third_ends(r):
-        for start, size in ends:
-            part[r + EDGE, pl.ds(start, size)] = advance(q2, r + EDGE, start, size)
-
-    sweep(depth - 2 * EDGE, 4, third_ends)
-    for r in (0, 1, depth - 2, depth - 1):
-        for start, size in whole:
-            part[r, pl.ds(start, size)] = advance(q2, r, start, size)
+    def second(spans):
+        def step(r):
+            for start, size in spans:
+                q2[r + EDGE, pl.ds(PAD + start, size)] = advance(q1, r, start, size)
+
+        return step
+
+    def third(spans):
+        def step(r):
+            for start, size in spans:
+                part[r, pl.ds(start, size)] = advance(q2, r, start, size)
+
+        return step
+
+    def outside(step, half):
+        sweep_from(EDGE + half * (half_depth - EDGE), half_depth - EDGE, 2, step(ends))
+        for r in (0, 1) if half == 0 else (depth - 2, depth - 1):
+            step(whole)(r)
+
+    sweep_from(EDGE, depth - 2 * EDGE, 2, second(middle))
+    wait_lat(q1, 1)
+    for half in range(2):
+        wait_lon(q1, 1, half)
+        outside(second, half)
+        start_lon(q2, 2, half)
+    start_lat(q2, 2)
+    sweep_from(EDGE, depth - 2 * EDGE, 2, third(middle))
+    wait_lat(q2, 2)
+    for half in range(2):
+        wait_lon(q2, 2, half)
+        outside(third, half)
+
     for step in range(STEPS):
-        to_east, to_west, to_north, to_south = halo_copies(step)
-        to_east.wait_send()
-        to_west.wait_send()
+        for half in range(2):
+            for copy in lon_copies(step, half):
+                copy.wait_send()
+        to_north, to_south = lat_copies(step)
 
         @pl.when(lat < 3)
         def _():
@@ -380,7 +396,7 @@
 
     across.wait_send()
     for h in range(2):
-        a = recv.at[pl.ds(h * PARTNERS + 1, PARTNERS - 1), pl.ds(0, used)]
+        a = recv.at[pl.ds(h * PARTNERS + 1, PARTNERS - 1), pl.ds(0, used[h])]
         pltpu.make_async_copy(a, a, send_sem.at[h]).wait()
 
 
@@ -426,9 +442,9 @@
             raw, coarse, coarse, coarse, vmem((levels, rows, columns), i32),
             vmem((fields, depth, BANDS, columns), f32), coarse,
             tall, tall, tall, turned, turned, turned, turned, turned,
-            vmem((STEPS, 2, EDGE * depth, 128), f32), vmem((STEPS, 2, EDGE * depth, 128), f32),
+            vmem((STEPS, 2, 2, EDGE * depth // 2, 128), f32), vmem((STEPS, 2, 2, EDGE * depth // 2, 128), f32),
             vmem((STEPS, 2, 16 * EDGE, 128), f32), vmem((STEPS, 2, 16 * EDGE, 128), f32),
-            dma((8,)), dma, pltpu.SemaphoreType.REGULAR((2,)), dma, dma, dma((2,)), dma((2,)), dma((STEPS, 4)), dma((STEPS, 4)),
+            dma((8,)), dma, pltpu.SemaphoreType.REGULAR((2,)), dma, dma, dma((2,)), dma((2,)), dma((STEPS, 6)), dma((STEPS, 6)),
         ],
         compiler_params=pltpu.CompilerParams(
             collective_id=0, has_side_effects=True, vmem_limit_bytes=VL << 20

time: 51.8 us -> 50.6 us (0.977); the launches traced: 50.9 us -> 50.4 us
  no operation moved by 1% of the time
where the time goes in v5:
time: 50.6 us; the launch traced here: 50.4 us
  Pallas kernels  50.4 us (100%)
    pallas_call x1, Pallas kernels, body(): pl.pallas_call(kernel, out_shape=jax.ShapeDtypeStruct((depth, columns, 12...  48 us
    pallas_call x1, Pallas kernels, body(): pl.pallas_call(turn_back, out_shape=jax.ShapeDtypeStruct((fields, BANDS,...  2.36 us

profile of v5, /device:TPU:1, one launch (start us, length us, event | category | flops | bytes accessed | tf_op | source)
XLA Modules:
  0.0 50.4 jit_solution(12337968757145604157)
XLA Ops:
  0.0 48.0 %shard_map.82.bands = f32[32,128,128]{2,1,0:T(8,128)S(1)} custom-call(f32[16,256,128]{2,1,0:T(8,128)} %bitcast.5, f32[128,16,128]{2,1,0:T(8,128)} %bitcast.6, s32[1,128]{1,0:T(1,128)} %bitcast.7, s32[1,128]{1,0:T(1,128)} %bitcast.8, f32[8,256,128]{2,1,0:T(8,128)} %kappa.1, f32[8,256,128]{2,1,0:T(8,128)} %lon_speed.1, f32[8,256,128]{2,1,0:T(8,128)} %lat_speed.1, ...), custom_call_target="tpu_custom_call" | custom-call | tf_op jit(solution)/shard_map/pallas_call | solution.py:432
  48.0 2.4 %shard_map.83 = f32[16,8,32,128]{3,2,1,0:T(8,128)} custom-call(f32[32,128,128]{2,1,0:T(8,128)S(1)} %shard_map.82.bands), custom_call_target="tpu_custom_call" | custom-call | tf_op jit(solution)/shard_map/pallas_call | solution.py:459

commit v6 on v5

--- a/solution.py
+++ b/solution.py
@@ -14,6 +14,7 @@
 VL = 44
 PAD = 8
 EDGE = 2
+PARTS = 4
 OFFSETS = sorted(
     ((z, x, y) for z in range(4) for x in range(4) for y in range(4)),
     key=lambda o: (sum(d > 0 for d in o), -sum(d == 2 for d in o), (16 * o[0] + 4 * o[1] + o[2]) * 27 % 64),
@@ -122,26 +123,26 @@
             device_id=device, device_id_type=MESH,
         )
 
-    def lon_copies(step, half):
+    def lon_copies(step, p):
         return [
-            halo_copy(lon_out.at[step, d, half], lon_in.at[step, d, half], step, 2 * half + d, device)
+            halo_copy(lon_out.at[step, d, p], lon_in.at[step, d, p], step, 2 * p + d, device)
             for d, device in enumerate((east, west))
         ]
 
     def lat_copies(step):
         return [
-            halo_copy(lat_out.at[step, d], lat_in.at[step, d], step, 4 + d, (lon, there))
+            halo_copy(lat_out.at[step, d], lat_in.at[step, d], step, 2 * PARTS + d, (lon, there))
             for d, there in enumerate((jnp.minimum(lat + 1, 3), jnp.maximum(lat - 1, 0)))
         ]
 
-    half_depth = depth // 2
-
-    def start_lon(q, step, half):
-        for k in range(half_depth):
-            n, at = EDGE + half * half_depth + k, pl.ds(EDGE * k, EDGE)
-            lon_out[step, 0, half, at] = q[n, pl.ds(PAD + columns - EDGE, EDGE)]
-            lon_out[step, 1, half, at] = q[n, pl.ds(PAD, EDGE)]
-        for copy in lon_copies(step, half):
+    some_rows = depth // PARTS
+
+    def start_lon(q, step, p):
+        for k in range(some_rows):
+            n, at = EDGE + p * some_rows + k, pl.ds(EDGE * k, EDGE)
+            lon_out[step, 0, p, at] = q[n, pl.ds(PAD + columns - EDGE, EDGE)]
+            lon_out[step, 1, p, at] = q[n, pl.ds(PAD, EDGE)]
+        for copy in lon_copies(step, p):
             copy.start()
 
     def start_lat(q, step):
@@ -167,13 +168,13 @@
         def _():
             to_south.start()
 
-    def wait_lon(q, step, half):
-        for copy in lon_copies(step, half):
+    def wait_lon(q, step, p):
+        for copy in lon_copies(step, p):
             copy.wait_recv()
-        for k in range(half_depth):
-            n, at = EDGE + half * half_depth + k, pl.ds(EDGE * k, EDGE)
-            q[n, pl.ds(PAD - EDGE, EDGE)] = lon_in[step, 0, half, at]
-            q[n, pl.ds(PAD + columns, EDGE)] = lon_in[step, 1, half, at]
+        for k in range(some_rows):
+            n, at = EDGE + p * some_rows + k, pl.ds(EDGE * k, EDGE)
+            q[n, pl.ds(PAD - EDGE, EDGE)] = lon_in[step, 0, p, at]
+            q[n, pl.ds(PAD + columns, EDGE)] = lon_in[step, 1, p, at]
 
     def wait_lat(q, step):
         to_north, to_south = lat_copies(step)
@@ -239,8 +240,8 @@
 
     sweep(depth, 4, turn_state)
 
-    for half in range(2):
-        start_lon(q0, 0, half)
+    for p in range(PARTS):
+        start_lon(q0, 0, p)
     start_lat(q0, 0)
     pl.semaphore_wait(line_sem.at[0], LINES - 1)
     for i in range(1, LINES):
@@ -296,8 +297,8 @@
     ends = [(0, 8), (columns - 8, 8)]
 
     wait_lat(q0, 0)
-    for half in range(2):
-        wait_lon(q0, 0, half)
+    for p in range(PARTS):
+        wait_lon(q0, 0, p)
 
     def first_step(r):
         for start, size in whole:
@@ -330,7 +331,7 @@
         both = jnp.dot(selector, jnp.concatenate([high, rest], axis=1), preferred_element_type=jnp.float32)
         raw_force[n] = (both[:, :columns] + both[:, columns:]).reshape(depth, BANDS, columns)
 
-    sweep(fields, 8, assemble)
+    sweep(fields, 16, assemble)
 
     def add_forcing(r):
         forcing = jnp.transpose(raw_force[:, r].reshape(fields * BANDS, columns)) * wet[r]
@@ -340,9 +341,9 @@
     def sweep_from(start, count, unroll, step):
         sweep(count, unroll, lambda r: step(r + start))
 
-    for half in range(2):
-        sweep_from(half * half_depth, half_depth, 4, add_forcing)
-        start_lon(q1, 1, half)
+    for p in range(PARTS):
+        sweep_from(p * some_rows, some_rows, min(some_rows, 8), add_forcing)
+        start_lon(q1, 1, p)
     start_lat(q1, 1)
 
     def advance(q, r, start, size):
@@ -362,27 +363,30 @@
 
         return step
 
-    def outside(step, half):
-        sweep_from(EDGE + half * (half_depth - EDGE), half_depth - EDGE, 2, step(ends))
-        for r in (0, 1) if half == 0 else (depth - 2, depth - 1):
-            step(whole)(r)
-
+    def outside(step, part_number):
+        sweep_from(part_number * some_rows, some_rows, min(some_rows, 8), step(ends))
+
+    edge_rows = (0, 1, depth - 2, depth - 1)
     sweep_from(EDGE, depth - 2 * EDGE, 2, second(middle))
     wait_lat(q1, 1)
-    for half in range(2):
-        wait_lon(q1, 1, half)
-        outside(second, half)
-        start_lon(q2, 2, half)
+    for r in edge_rows:
+        second(middle)(r)
+    for p in range(PARTS):
+        wait_lon(q1, 1, p)
+        outside(second, p)
+        start_lon(q2, 2, p)
     start_lat(q2, 2)
     sweep_from(EDGE, depth - 2 * EDGE, 2, third(middle))
     wait_lat(q2, 2)
-    for half in range(2):
-        wait_lon(q2, 2, half)
-        outside(third, half)
+    for r in edge_rows:
+        third(middle)(r)
+    for p in range(PARTS):
+        wait_lon(q2, 2, p)
+        outside(third, p)
 
     for step in range(STEPS):
-        for half in range(2):
-            for copy in lon_copies(step, half):
+        for p in range(PARTS):
+            for copy in lon_copies(step, p):
                 copy.wait_send()
         to_north, to_south = lat_copies(step)
 
@@ -442,9 +446,9 @@
             raw, coarse, coarse, coarse, vmem((levels, rows, columns), i32),
             vmem((fields, depth, BANDS, columns), f32), coarse,
             tall, tall, tall, turned, turned, turned, turned, turned,
-            vmem((STEPS, 2, 2, EDGE * depth // 2, 128), f32), vmem((STEPS, 2, 2, EDGE * depth // 2, 128), f32),
+            vmem((STEPS, 2, PARTS, EDGE * depth // PARTS, 128), f32), vmem((STEPS, 2, PARTS, EDGE * depth // PARTS, 128), f32),
             vmem((STEPS, 2, 16 * EDGE, 128), f32), vmem((STEPS, 2, 16 * EDGE, 128), f32),
-            dma((8,)), dma, pltpu.SemaphoreType.REGULAR((2,)), dma, dma, dma((2,)), dma((2,)), dma((STEPS, 6)), dma((STEPS, 6)),
+            dma((8,)), dma, pltpu.SemaphoreType.REGULAR((2,)), dma, dma, dma((2,)), dma((2,)), dma((STEPS, 2 * PARTS + 2)), dma((STEPS, 2 * PARTS + 2)),
         ],
         compiler_params=pltpu.CompilerParams(
             collective_id=0, has_side_effects=True, vmem_limit_bytes=VL << 20

time: 50.6 us -> 49.4 us (0.976)
  Pallas kernels: 50.4 us -> 49.2 us
    pallas_call x1, Pallas kernels: 48 us -> 46.8 us  [body(): pl.pallas_call(kernel, out_shape=jax.ShapeDtypeStruct((depth, columns, 12...]
where the time goes in v6:
time: 49.4 us; the launch traced here: 49.2 us
  Pallas kernels  49.2 us (100%)
    pallas_call x1, Pallas kernels, body(): pl.pallas_call(kernel, out_shape=jax.ShapeDtypeStruct((depth, columns, 12...  46.8 us
    pallas_call x1, Pallas kernels, body(): pl.pallas_call(turn_back, out_shape=jax.ShapeDtypeStruct((fields, BANDS,...  2.36 us

profile of v6, /device:TPU:1, one launch (start us, length us, event | category | flops | bytes accessed | tf_op | source)
XLA Modules:
  0.0 49.2 jit_solution(4923389242544933547)
XLA Ops:
  0.0 46.8 %shard_map.82.bands = f32[32,128,128]{2,1,0:T(8,128)S(1)} custom-call(f32[16,256,128]{2,1,0:T(8,128)} %bitcast.5, f32[128,16,128]{2,1,0:T(8,128)} %bitcast.6, s32[1,128]{1,0:T(1,128)} %bitcast.7, s32[1,128]{1,0:T(1,128)} %bitcast.8, f32[8,256,128]{2,1,0:T(8,128)} %kappa.1, f32[8,256,128]{2,1,0:T(8,128)} %lon_speed.1, f32[8,256,128]{2,1,0:T(8,128)} %lat_speed.1, ...), custom_call_target="tpu_custom_call" | custom-call | tf_op jit(solution)/shard_map/pallas_call | solution.py:436
  46.9 2.4 %shard_map.83 = f32[16,8,32,128]{3,2,1,0:T(8,128)} custom-call(f32[32,128,128]{2,1,0:T(8,128)S(1)} %shard_map.82.bands), custom_call_target="tpu_custom_call" | custom-call | tf_op jit(solution)/shard_map/pallas_call | solution.py:463

commit v7 on v6

--- a/solution.py
+++ b/solution.py
@@ -20,6 +20,8 @@
     key=lambda o: (sum(d > 0 for d in o), -sum(d == 2 for d in o), (16 * o[0] + 4 * o[1] + o[2]) * 27 % 64),
 )
 LINES, PLANES = 10, 37
+Z_LINE = [i for i in range(1, LINES) if OFFSETS[i][0] > 0]
+X_LINE = [i for i in range(1, LINES) if OFFSETS[i][1] > 0]
 
 
 def roll(x, amount):
@@ -57,13 +59,13 @@
         (lat_speed, raw_merid.at[pl.ds(0, levels)]), (mask, raw_wet),
     )
     loads = [pltpu.make_async_copy(src, dst, load_sem.at[k]) for k, (src, dst) in enumerate(moves)]
-    for copy in loads[:4]:
-        copy.start()
     east, west = ((lon + 1) % 32, lat), ((lon + 31) % 32, lat)
 
     barrier = pltpu.get_barrier_semaphore()
     for device in [partner(i) for i in range(1, LINES)] + [other, (lon, 3 - lat), east, west]:
         pl.semaphore_signal(barrier, inc=1, device_id=device, device_id_type=MESH)
+    for copy in loads[:4]:
+        copy.start()
     loads[0].wait()
     loads[1].wait()
 
@@ -225,7 +227,7 @@
             ).start()
 
     pl.semaphore_wait(barrier, LINES + 3)
-    for i in range(1, LINES):
+    for i in Z_LINE + X_LINE:
         pl.semaphore_signal(line_sem.at[0], inc=1, device_id=partner(i), device_id_type=MESH)
     across.start()
     post(0, range(1, LINES))
@@ -238,16 +240,16 @@
     def turn_state(r):
         q0[r + EDGE, inner] = turned(raw_state, r)
 
-    sweep(depth, 4, turn_state)
+    sweep(depth, 8, turn_state)
 
     for p in range(PARTS):
         start_lon(q0, 0, p)
     start_lat(q0, 0)
-    pl.semaphore_wait(line_sem.at[0], LINES - 1)
-    for i in range(1, LINES):
+    pl.semaphore_wait(line_sem.at[0], len(Z_LINE + X_LINE))
+    for i in Z_LINE:
         pl.semaphore_signal(line_sem.at[1], inc=1, device_id=partner(i), device_id_type=MESH)
     post(0, range(LINES, PLANES))
-    pl.semaphore_wait(line_sem.at[1], LINES - 1)
+    pl.semaphore_wait(line_sem.at[1], len(Z_LINE))
     post(0, range(PLANES, PARTNERS))
     across.wait_recv()
     for i in range(PARTNERS):
@@ -277,7 +279,7 @@
         def turn(r):
             ref[r] = turned(raw, r)
 
-        sweep(depth, 4, turn)
+        sweep(depth, 8, turn)
 
     def stencil(q, r, start, size):
         n, here_at = r + EDGE, pl.ds(PAD + start, size)
@@ -367,7 +369,7 @@
         sweep_from(part_number * some_rows, some_rows, min(some_rows, 8), step(ends))
 
     edge_rows = (0, 1, depth - 2, depth - 1)
-    sweep_from(EDGE, depth - 2 * EDGE, 2, second(middle))
+    sweep_from(EDGE, depth - 2 * EDGE, 4, second(middle))
     wait_lat(q1, 1)
     for r in edge_rows:
         second(middle)(r)
@@ -376,7 +378,7 @@
         outside(second, p)
         start_lon(q2, 2, p)
     start_lat(q2, 2)
-    sweep_from(EDGE, depth - 2 * EDGE, 2, third(middle))
+    sweep_from(EDGE, depth - 2 * EDGE, 4, third(middle))
     wait_lat(q2, 2)
     for r in edge_rows:
         third(middle)(r)

time: 49.4 us -> 49.4 us (level)
  no operation moved by 1% of the time
where the time goes in v7:
time: 49.4 us; the launch traced here: 49.3 us
  Pallas kernels  49.3 us (100%)
    pallas_call x1, Pallas kernels, body(): pl.pallas_call(kernel, out_shape=jax.ShapeDtypeStruct((depth, columns, 12...  46.9 us
    pallas_call x1, Pallas kernels, body(): pl.pallas_call(turn_back, out_shape=jax.ShapeDtypeStruct((fields, BANDS,...  2.36 us

profile of v7, /device:TPU:1, one launch (start us, length us, event | category | flops | bytes accessed | tf_op | source)
XLA Modules:
  0.0 49.3 jit_solution(1836242534380311144)
XLA Ops:
  0.0 46.9 %shard_map.82.bands = f32[32,128,128]{2,1,0:T(8,128)S(1)} custom-call(f32[16,256,128]{2,1,0:T(8,128)} %bitcast.5, f32[128,16,128]{2,1,0:T(8,128)} %bitcast.6, s32[1,128]{1,0:T(1,128)} %bitcast.7, s32[1,128]{1,0:T(1,128)} %bitcast.8, f32[8,256,128]{2,1,0:T(8,128)} %kappa.1, f32[8,256,128]{2,1,0:T(8,128)} %lon_speed.1, f32[8,256,128]{2,1,0:T(8,128)} %lat_speed.1, ...), custom_call_target="tpu_custom_call" | custom-call | tf_op jit(solution)/shard_map/pallas_call | solution.py:438
  46.9 2.4 %shard_map.83 = f32[16,8,32,128]{3,2,1,0:T(8,128)} custom-call(f32[32,128,128]{2,1,0:T(8,128)S(1)} %shard_map.82.bands), custom_call_target="tpu_custom_call" | custom-call | tf_op jit(solution)/shard_map/pallas_call | solution.py:465
